TPU v7x, 128 devices: a whole 4x4x4 slice. The times are simulated.
128 devices in a mesh: ctx: 16 (over y, x), tp: 8 (over z, core).
Axes of the slice: x: 4, y: 4, z: 4, core: 2. Of those that a mesh axis runs over, the one named last changes fastest.
Arguments:
- hidden_in: bfloat16 [8192, 2048], P('ctx'), may hold values from -6 to 6
- norm_gains: float32 [2, 2048], replicated, may hold values from 0.5 to 1.5
- w_in: bfloat16 [2048, 8, 896], P(None, 'tp'), may hold values from -0.125 to 0.125
- w_shared: bfloat16 [2048, 1024], replicated, may hold values from -0.125 to 0.125
- w_dt: bfloat16 [2048, 48], P(None, 'tp'), may hold values from -0.125 to 0.125
- head_params: float32 [3, 48], P(None, 'tp'), as said below
- w_out: bfloat16 [8, 512, 2048], P('tp'), may hold values from -0.25 to 0.25
- w_gu: bfloat16 [2048, 2, 4096], P(None, None, 'tp'), may hold values from -0.125 to 0.125
- w_down: bfloat16 [4096, 2048], P('tp'), may hold values from -0.09375 to 0.09375
- a_in: bfloat16 [2048, 128], replicated, may hold values from -0.125 to 0.125
- b_in: bfloat16 [128, 8, 896], P(None, 'tp'), may hold values from -0.75 to 0.75
- a_sh: bfloat16 [2048, 128], replicated, may hold values from -0.125 to 0.125
- b_sh: bfloat16 [128, 1024], replicated, may hold values from -0.75 to 0.75
- a_out: bfloat16 [8, 512, 128], P('tp'), may hold values from -0.125 to 0.125
- b_out: bfloat16 [128, 2048], replicated, may hold values from -0.75 to 0.75
- a_gu: bfloat16 [2048, 128], replicated, may hold values from -0.125 to 0.125
- b_gu: bfloat16 [128, 2, 4096], P(None, None, 'tp'), may hold values from -0.75 to 0.75
- a_dn: bfloat16 [4096, 128], P('tp'), may hold values from -0.09375 to 0.09375
- b_dn: bfloat16 [128, 2048], replicated, may hold values from -0.75 to 0.75
- adapter_ids: int32 [4], replicated, may hold values from 0 to 7
- doc_lengths: int32 [4], replicated, may hold values from 1 to 7936, 8192 in all
- out_grad: bfloat16 [8192, 2048], P('ctx'), may hold values from -6 to 6
Outputs:
- mixed: float32 [8192, 2048], P('ctx')
- input_grad: float32 [8192, 2048], P('ctx')
- grad_norm_gains: float32 [2, 2048], P(None, 'ctx')
- grad_w_in: float32 [2048, 8, 896], P('ctx', 'tp')
- grad_w_shared: float32 [2048, 1024], P('ctx')
- grad_w_dt: float32 [2048, 48], P('ctx', 'tp')
- grad_head_params: float32 [3, 48], P(None, 'tp')
- grad_w_out: float32 [8, 512, 2048], P('tp', None, 'ctx')
- grad_w_gu: float32 [2048, 2, 4096], P('ctx', None, 'tp')
- grad_w_down: float32 [4096, 2048], P('tp', 'ctx')
- grad_a_in: float32 [2048, 128], P(('ctx', 'tp'))
- grad_b_in: float32 [128, 8, 896], P('ctx', 'tp')
- grad_a_sh: float32 [2048, 128], P('ctx')
- grad_b_sh: float32 [128, 1024], P('ctx')
- grad_a_out: float32 [8, 512, 128], P('tp', 'ctx')
- grad_b_out: float32 [128, 2048], P(None, ('ctx', 'tp'))
- grad_a_gu: float32 [2048, 128], P(('ctx', 'tp'))
- grad_b_gu: float32 [128, 2, 4096], P('ctx', None, 'tp')
- grad_a_dn: float32 [4096, 128], P('tp', 'ctx')
- grad_b_dn: float32 [128, 2048], P(None, ('ctx', 'tp'))
Inputs may be any that keep to these rules, and one draw needn't show every extreme that they name: `doc_lengths`: the lengths sum to 8192; one sequence is 7936 tokens long. `head_params`: row 0: step biases, row 1: logarithms of decay scales, row 2: skip factors.
All inputs are finite; a program needn't handle non-finite values.
Results may differ from a plain program's by a relative error of at most 0.03.
Values may be sent and summed in bfloat16 or wider, within the bound.
A program may use at most 192 MiB of HBM per device.

v0:
```python
import jax
import jax.numpy as jnp
from jax import lax
from jax.sharding import PartitionSpec as P

MHEAD = 64
STATE = 256
QHEADS = 8
KVH = 2
HD = 128
RANK = 16


NORM_EPSILON = 1e-06


def prefix(value, axis, combine, identity):
    length, mine = (lax.axis_size(axis), lax.axis_index(axis))
    everything = jax.tree.map(
        lambda part, kind: lax.all_gather(part.astype(kind), axis),
        value,
        (jnp.bfloat16, jnp.bfloat16),
    )
    start = jax.tree.map(
        lambda part, zero: jnp.broadcast_to(jnp.asarray(zero, part.dtype), part.shape),
        value,
        identity,
    )

    def lap(k, before):
        reached = k < mine
        new = combine(
            before, jax.tree.map(lambda part, own: part[k].astype(own.dtype), everything, value)
        )
        return jax.tree.map(lambda a, b: jnp.where(reached, a, b), new, before)

    return lax.fori_loop(0, length, lap, start)


def prefix_2(value, axis, combine, identity):
    length, mine = (lax.axis_size(axis), lax.axis_index(axis))
    everything = jax.tree.map(
        lambda part, kind: lax.all_gather(part.astype(kind), axis),
        value,
        jax.tree.map(lambda a: jnp.bfloat16 if a.dtype == jnp.float32 else a.dtype, value),
    )
    start = jax.tree.map(
        lambda part, zero: jnp.broadcast_to(jnp.asarray(zero, part.dtype), part.shape),
        value,
        identity,
    )

    def lap(k, before):
        at = length - 1 - k
        reached = at > mine
        new = combine(
            before, jax.tree.map(lambda part, own: part[at].astype(own.dtype), everything, value)
        )
        return jax.tree.map(lambda a, b: jnp.where(reached, a, b), new, before)

    return lax.fori_loop(0, length, lap, start)


def exact_dot(left_side, right_side):
    return jnp.dot(
        left_side, right_side, precision=lax.Precision.HIGH, preferred_element_type=jnp.float32
    )


def plain_dot(left_side, right_side):
    return jnp.dot(left_side, right_side, preferred_element_type=jnp.float32)


def norm_apply(values, gain_row):
    return (
        values
        * lax.rsqrt(jnp.mean(values * values, axis=-1, keepdims=True) + NORM_EPSILON)
        * gain_row
    )


def soft_plus(values):
    return jnp.maximum(values, 0.0) + jnp.log1p(jnp.exp(-jnp.abs(values)))


def doc_index(positions, doc_lengths):
    bounds = jnp.cumsum(doc_lengths)
    return jnp.sum((positions[:, None] >= bounds[None, :]).astype(jnp.int32), axis=1)


def adapter_mask(doc_ids, adapter_ids, columns):
    seq_count = adapter_ids.shape[0]
    chosen = jnp.sum(
        jnp.where(doc_ids[:, None] == jnp.arange(seq_count)[None, :], adapter_ids[None, :], 0),
        axis=1,
    )
    return (chosen[:, None] == jnp.arange(columns)[None, :] // RANK).astype(jnp.float32)


def decay_terms(dt_raw, head_params):
    step_size = soft_plus(dt_raw + head_params[0])
    return (step_size, jnp.cumsum(-step_size * jnp.exp(head_params[1]), axis=0))


def ssd_inner(values, b_matrix, dt_raw, head_params, doc_ids, doc_before, intersection):
    step_size, decay_sum = decay_terms(dt_raw, head_params)
    row_order = jnp.arange(values.shape[0])
    allowed = (row_order[:, None] >= row_order[None, :]) & (doc_ids[:, None] == doc_ids[None, :])
    decay_gap = jnp.where(allowed[:, :, None], decay_sum[:, None, :] - decay_sum[None, :, :], 0.0)
    weights = jnp.where(allowed[:, :, None], jnp.exp(decay_gap), 0.0) * step_size[None, :, :]
    mixing = intersection[:, :, None] * weights
    output = jnp.einsum("tsh,shp->thp", mixing, values, precision=lax.Precision.HIGH)
    output = output + head_params[2][None, :, None] * values
    tail_weight = (
        jnp.where(
            (doc_ids == doc_ids[-1])[:, None], jnp.exp(decay_sum[-1][None, :] - decay_sum), 0.0
        )
        * step_size
    )
    state_out = jnp.einsum(
        "sn,shp->hnp", b_matrix, tail_weight[:, :, None] * values, precision=lax.Precision.HIGH
    )
    carried = (doc_ids[-1] == doc_before).astype(values.dtype)
    return (output, state_out, jnp.exp(decay_sum[-1]) * carried)


def ssd_cross(c_matrix, dt_raw, head_params, entering, doc_ids, doc_before):
    step_size, decay_sum = decay_terms(dt_raw, head_params)
    carried = (doc_ids == doc_before).astype(c_matrix.dtype)
    reach_weight = jnp.exp(decay_sum) * carried[:, None]
    return (
        jnp.einsum("tn,hnp->thp", c_matrix, entering, precision=lax.Precision.HIGH)
        * reach_weight[:, :, None]
    )


def forward_combine(earlier_part, later_part):
    return (
        earlier_part[0] * later_part[0],
        later_part[0][:, None, None] * earlier_part[1] + later_part[1],
    )


def backward_combine(earlier_part, later_part):
    return (
        earlier_part[0] * later_part[0],
        later_part[1] + later_part[0][:, None, None] * earlier_part[1],
    )


def body(
    hidden_in,
    norm_gains,
    w_in,
    w_shared,
    w_dt,
    head_params,
    w_out,
    w_gu,
    w_down,
    a_in,
    b_in,
    a_sh,
    b_sh,
    a_out,
    b_out,
    a_gu,
    b_gu,
    a_dn,
    b_dn,
    adapter_ids,
    doc_lengths,
    out_grad,
):
    row_count, model_width = hidden_in.shape
    head_count = head_params.shape[1]
    inner_width = head_count * MHEAD
    tp_count = lax.axis_size("tp")
    q_heads = QHEADS // tp_count
    ctx_at = lax.axis_index("ctx")
    tp_at = lax.axis_index("tp")
    positions = ctx_at * row_count + jnp.arange(row_count, dtype=jnp.int32)
    doc_ids = doc_index(positions, doc_lengths)
    doc_before = doc_index(jnp.maximum(positions[:1] - 1, 0), doc_lengths)[0]
    adapter_rows = adapter_mask(doc_ids, adapter_ids, a_in.shape[1])
    w_in_flat = w_in.reshape(model_width, -1)
    b_in_flat = b_in.reshape(b_in.shape[0], -1)
    w_out_flat = w_out.reshape(-1, model_width)
    a_out_flat = a_out.reshape(-1, a_out.shape[2])
    w_gu_flat = w_gu.reshape(model_width, -1)
    b_gu_flat = b_gu.reshape(b_gu.shape[0], -1)
    hidden_units = w_down.shape[0]
    scale_factor = HD ** (-0.5)
    source = hidden_in.astype(jnp.float32)
    gain_one = norm_gains[0]
    gain_two = norm_gains[1]
    normed_one = norm_apply(source, gain_one).astype(jnp.bfloat16)
    low_in = plain_dot(normed_one, a_in) * adapter_rows
    h_one = (
        plain_dot(normed_one, w_in_flat) + exact_dot(low_in, b_in_flat.astype(jnp.float32))
    ).astype(jnp.bfloat16)
    low_sh = plain_dot(normed_one, a_sh) * adapter_rows
    h_two = (plain_dot(normed_one, w_shared) + exact_dot(low_sh, b_sh.astype(jnp.float32))).astype(
        jnp.bfloat16
    )
    dt_raw = plain_dot(normed_one, w_dt)
    gate_ssm = h_one[:, :inner_width].astype(jnp.float32)
    values = (
        h_one[:, inner_width : 2 * inner_width]
        .astype(jnp.float32)
        .reshape(row_count, head_count, MHEAD)
    )
    queries = h_one[:, 2 * inner_width :].reshape(row_count, q_heads, HD).transpose(1, 0, 2)
    b_rounded = h_two[:, :STATE]
    c_rounded = h_two[:, STATE : 2 * STATE]
    b_matrix = b_rounded.astype(jnp.float32)
    c_matrix = c_rounded.astype(jnp.float32)
    intersection = plain_dot(c_rounded, b_rounded.T)
    kv_group = tp_at * q_heads // (QHEADS // KVH)
    key_col = 2 * STATE + kv_group * HD
    keys_mine = lax.dynamic_slice_in_dim(h_two, key_col, HD, 1)
    vals_mine = lax.dynamic_slice_in_dim(h_two, key_col + KVH * HD, HD, 1)
    inner_out, state_out, decay_total = ssd_inner(
        values, b_matrix, dt_raw, head_params, doc_ids, doc_before, intersection
    )
    state_ident = (jnp.ones_like(decay_total), jnp.zeros_like(state_out))
    _, entering = prefix((decay_total, state_out), "ctx", forward_combine, state_ident)
    ssd_out = inner_out + ssd_cross(c_matrix, dt_raw, head_params, entering, doc_ids, doc_before)
    run_top = jnp.full((q_heads, row_count), -1e30, jnp.float32)
    key_piece = lax.all_gather(keys_mine, "ctx", axis=0, tiled=True)
    value_piece = lax.all_gather(vals_mine, "ctx", axis=0, tiled=True)
    key_pos = jnp.arange(key_piece.shape[0], dtype=jnp.int32)
    key_docs = doc_index(key_pos, doc_lengths)
    allowed = (positions[:, None] >= key_pos[None, :]) & (doc_ids[:, None] == key_docs[None, :])
    scores = (
        jnp.einsum("hrd,nd->hrn", queries, key_piece, preferred_element_type=jnp.float32)
        * scale_factor
    )
    scores = jnp.where(allowed[None], scores, -1e30)
    new_top = jnp.maximum(run_top, jnp.max(scores, axis=-1))
    weights = jnp.where(allowed[None], jnp.exp(scores - new_top[:, :, None]), 0.0)
    run_total = jnp.sum(weights, axis=-1)
    run_acc = jnp.einsum(
        "hrn,nd->hrd", weights.astype(jnp.bfloat16), value_piece, preferred_element_type=jnp.float32
    )
    run_top, run_total, run_acc = (new_top, run_total, run_acc)
    log_total = run_top + jnp.log(run_total)
    attn_out = run_acc / run_total[:, :, None]
    ssd_flat = ssd_out.reshape(row_count, inner_width)
    gate_sig = jax.nn.sigmoid(gate_ssm)
    gated = ssd_flat * (gate_ssm * gate_sig)
    attn_flat = attn_out.transpose(1, 0, 2).reshape(row_count, q_heads * HD)
    merged = jnp.concatenate([gated, attn_flat], axis=1).astype(jnp.bfloat16)
    low_out = plain_dot(merged, a_out_flat) * adapter_rows
    mix_part = plain_dot(merged, w_out_flat) + exact_dot(low_out, b_out.astype(jnp.float32))
    mixer_out = lax.psum(mix_part.astype(jnp.bfloat16), "tp").astype(jnp.float32)
    residual = source + mixer_out
    normed_two = norm_apply(residual, gain_two).astype(jnp.bfloat16)
    low_gu = plain_dot(normed_two, a_gu) * adapter_rows
    h_gu = (
        plain_dot(normed_two, w_gu_flat) + exact_dot(low_gu, b_gu_flat.astype(jnp.float32))
    ).astype(jnp.bfloat16)
    gate_mlp = h_gu[:, :hidden_units].astype(jnp.float32)
    up_mlp = h_gu[:, hidden_units:].astype(jnp.float32)
    sig_mlp = jax.nn.sigmoid(gate_mlp)
    act_mlp = (gate_mlp * sig_mlp * up_mlp).astype(jnp.bfloat16)
    low_dn = plain_dot(act_mlp, a_dn) * adapter_rows
    mlp_part = plain_dot(act_mlp, w_down) + exact_dot(low_dn, b_dn.astype(jnp.float32))
    mlp_out = lax.psum(mlp_part.astype(jnp.bfloat16), "tp").astype(jnp.float32)
    mixed = residual + mlp_out
    grad_low_dn = plain_dot(out_grad, b_dn.T) * adapter_rows
    grad_act = (
        (plain_dot(out_grad, w_down.T) + exact_dot(grad_low_dn, a_dn.astype(jnp.float32).T))
        .astype(jnp.bfloat16)
        .astype(jnp.float32)
    )
    grad_gate = grad_act * up_mlp * sig_mlp * (1.0 + gate_mlp * (1.0 - sig_mlp))
    grad_up = grad_act * (gate_mlp * sig_mlp)
    grad_gu = jnp.concatenate([grad_gate, grad_up], axis=1).astype(jnp.bfloat16)
    grad_low_gu = plain_dot(grad_gu, b_gu_flat.T) * adapter_rows
    grad_normed_two = plain_dot(grad_gu, w_gu_flat.T) + exact_dot(
        grad_low_gu, a_gu.astype(jnp.float32).T
    )
    grad_normed_two = lax.psum(grad_normed_two.astype(jnp.bfloat16), "tp").astype(jnp.float32)
    _, norm_pull_two = jax.vjp(norm_apply, residual, gain_two)
    grad_resid_norm, grad_gain_two = norm_pull_two(grad_normed_two)
    grad_residual = out_grad.astype(jnp.float32) + grad_resid_norm
    grad_mixer = grad_residual.astype(jnp.bfloat16)
    grad_low_out = plain_dot(grad_mixer, b_out.T) * adapter_rows
    grad_merged = (
        plain_dot(grad_mixer, w_out_flat.T)
        + exact_dot(grad_low_out, a_out_flat.astype(jnp.float32).T)
    ).astype(jnp.bfloat16)
    grad_gated = grad_merged[:, :inner_width].astype(jnp.float32)
    grad_attn = grad_merged[:, inner_width:].reshape(row_count, q_heads, HD).transpose(1, 0, 2)
    grad_ssd = (grad_gated * (gate_ssm * gate_sig)).reshape(row_count, head_count, MHEAD)
    grad_gate_ssm = grad_gated * ssd_flat * gate_sig * (1.0 + gate_ssm * (1.0 - gate_sig))

    def ssd_full(vals_in, bmat_in, cmat_in, raw_in, params_in, enter_in, intersection_in):
        out_local, state_local, total_local = ssd_inner(
            vals_in, bmat_in, raw_in, params_in, doc_ids, doc_before, intersection_in
        )
        return (
            out_local + ssd_cross(cmat_in, raw_in, params_in, enter_in, doc_ids, doc_before),
            state_local,
            total_local,
        )

    _, ssd_pull = jax.vjp(
        ssd_full, values, b_matrix, c_matrix, dt_raw, head_params, entering, intersection
    )
    pull_first = ssd_pull((grad_ssd, jnp.zeros_like(state_out), jnp.zeros_like(decay_total)))
    _, grad_next = prefix_2((decay_total, pull_first[5]), "ctx", backward_combine, state_ident)
    pull_second = ssd_pull(
        (jnp.zeros_like(grad_ssd), grad_next, jnp.sum(grad_next * entering, axis=(1, 2)))
    )
    grad_intersection = pull_first[6] + pull_second[6]
    grad_values = pull_first[0] + pull_second[0]
    grad_bmat = pull_first[1] + pull_second[1] + exact_dot(grad_intersection.T, c_matrix)
    grad_cmat = pull_first[2] + pull_second[2] + exact_dot(grad_intersection, b_matrix)
    grad_dt = pull_first[3] + pull_second[3]
    grad_params = pull_first[4] + pull_second[4]
    grad_attn_f = grad_attn.astype(jnp.float32)
    delta_rows = jnp.sum(grad_attn_f * attn_out, axis=-1)
    key_all, value_all = (
        lax.all_gather(keys_mine, "ctx", axis=0, tiled=True),
        lax.all_gather(vals_mine, "ctx", axis=0, tiled=True),
    )
    key_total = key_all.shape[0]
    block_size = min(key_total, 512)
    block_count = key_total // block_size

    def back_block(grad_query, pieces):
        key_piece, value_piece, block_at = pieces
        key_pos = block_at * block_size + jnp.arange(block_size, dtype=jnp.int32)
        key_docs = doc_index(key_pos, doc_lengths)
        allowed = (positions[:, None] >= key_pos[None, :]) & (doc_ids[:, None] == key_docs[None, :])
        scores = (
            jnp.einsum("hrd,nd->hrn", queries, key_piece, preferred_element_type=jnp.float32)
            * scale_factor
        )
        probs = jnp.exp(jnp.where(allowed[None], scores - log_total[:, :, None], -1e30))
        grad_probs = jnp.einsum(
            "hrd,nd->hrn", grad_attn, value_piece, preferred_element_type=jnp.float32
        )
        grad_scores = (probs * (grad_probs - delta_rows[:, :, None])).astype(jnp.bfloat16)
        grad_query = grad_query + jnp.einsum(
            "hrn,nd->hrd", grad_scores, key_piece, preferred_element_type=jnp.float32
        )
        key_term = (
            jnp.einsum("hrn,hrd->nd", grad_scores, queries, preferred_element_type=jnp.float32)
            * scale_factor
        )
        value_term = jnp.einsum(
            "hrn,hrd->nd", probs.astype(jnp.bfloat16), grad_attn, preferred_element_type=jnp.float32
        )
        return (grad_query, (key_term, value_term))

    grad_query, (key_terms, value_terms) = lax.scan(
        back_block,
        jnp.zeros((q_heads, row_count, HD), jnp.float32),
        (
            key_all.reshape(block_count, block_size, HD),
            value_all.reshape(block_count, block_size, HD),
            jnp.arange(block_count, dtype=jnp.int32),
        ),
    )
    grad_keys, grad_vals = (
        lax.psum_scatter(
            key_terms.reshape(key_total, HD).astype(jnp.bfloat16),
            "ctx",
            scatter_dimension=0,
            tiled=True,
        ).astype(jnp.float32),
        lax.psum_scatter(
            value_terms.reshape(key_total, HD).astype(jnp.bfloat16),
            "ctx",
            scatter_dimension=0,
            tiled=True,
        ).astype(jnp.float32),
    )
    grad_query_flat = (
        (grad_query * scale_factor).transpose(1, 0, 2).reshape(row_count, q_heads * HD)
    )
    grad_one = jnp.concatenate(
        [grad_gate_ssm, grad_values.reshape(row_count, inner_width), grad_query_flat], axis=1
    ).astype(jnp.bfloat16)
    grad_two = jnp.concatenate(
        [grad_bmat, grad_cmat, jnp.zeros((row_count, 2 * KVH * HD), jnp.float32)], axis=1
    )
    grad_two = lax.dynamic_update_slice_in_dim(grad_two, grad_keys, key_col, 1)
    grad_two = lax.dynamic_update_slice_in_dim(grad_two, grad_vals, key_col + KVH * HD, 1)
    grad_low_in = plain_dot(grad_one, b_in_flat.T) * adapter_rows
    grad_norm_part = (
        plain_dot(grad_one, w_in_flat.T)
        + exact_dot(grad_low_in, a_in.astype(jnp.float32).T)
        + exact_dot(grad_dt, w_dt.astype(jnp.float32).T)
    )
    grad_norm_sum, grad_two = (
        lax.psum(grad_norm_part.astype(jnp.bfloat16), "tp").astype(jnp.float32),
        lax.psum(grad_two.astype(jnp.bfloat16), "tp").astype(jnp.float32),
    )
    grad_two_low = grad_two.astype(jnp.bfloat16)
    grad_low_sh = plain_dot(grad_two_low, b_sh.T) * adapter_rows
    grad_normed_one = (
        grad_norm_sum
        + plain_dot(grad_two_low, w_shared.T)
        + exact_dot(grad_low_sh, a_sh.astype(jnp.float32).T)
    )
    _, norm_pull_one = jax.vjp(norm_apply, source, gain_one)
    grad_source, grad_gain_one = norm_pull_one(grad_normed_one)
    input_grad = grad_residual + grad_source
    normed_one_f = normed_one.astype(jnp.float32)
    normed_two_f = normed_two.astype(jnp.float32)
    g_norm = jnp.stack([grad_gain_one, grad_gain_two])
    g_w_in = plain_dot(normed_one.T, grad_one).reshape(w_in.shape)
    g_b_in = exact_dot(low_in.T, grad_one.astype(jnp.float32)).reshape(b_in.shape)
    g_a_in = exact_dot(normed_one_f.T, grad_low_in)
    g_shared = plain_dot(normed_one.T, grad_two_low)
    g_b_sh = exact_dot(low_sh.T, grad_two_low.astype(jnp.float32))
    g_a_sh = exact_dot(normed_one_f.T, grad_low_sh)
    g_w_dt = exact_dot(normed_one_f.T, grad_dt)
    g_w_out = plain_dot(merged.T, grad_mixer).reshape(w_out.shape)
    g_b_out = exact_dot(low_out.T, grad_mixer.astype(jnp.float32))
    g_a_out = exact_dot(merged.astype(jnp.float32).T, grad_low_out).reshape(a_out.shape)
    g_w_gu = plain_dot(normed_two.T, grad_gu).reshape(w_gu.shape)
    g_b_gu = exact_dot(low_gu.T, grad_gu.astype(jnp.float32)).reshape(b_gu.shape)
    g_a_gu = exact_dot(normed_two_f.T, grad_low_gu)
    g_w_down = plain_dot(act_mlp.T, out_grad)
    g_b_dn = exact_dot(low_dn.T, out_grad.astype(jnp.float32))
    g_a_dn = exact_dot(act_mlp.astype(jnp.float32).T, grad_low_dn)
    grad_head = lax.psum(grad_params, "ctx")
    reduced = (
        lax.psum_scatter(
            g_norm.astype(jnp.bfloat16), "ctx", scatter_dimension=1, tiled=True
        ).astype(jnp.float32),
        lax.psum_scatter(
            g_w_in.astype(jnp.bfloat16), "ctx", scatter_dimension=0, tiled=True
        ).astype(jnp.float32),
        lax.psum_scatter(
            g_w_dt.astype(jnp.bfloat16), "ctx", scatter_dimension=0, tiled=True
        ).astype(jnp.float32),
        lax.psum_scatter(
            g_w_out.astype(jnp.bfloat16), "ctx", scatter_dimension=2, tiled=True
        ).astype(jnp.float32),
        lax.psum_scatter(
            g_w_gu.astype(jnp.bfloat16), "ctx", scatter_dimension=0, tiled=True
        ).astype(jnp.float32),
        lax.psum_scatter(
            g_w_down.astype(jnp.bfloat16), "ctx", scatter_dimension=1, tiled=True
        ).astype(jnp.float32),
        lax.psum_scatter(
            g_b_in.astype(jnp.bfloat16), "ctx", scatter_dimension=0, tiled=True
        ).astype(jnp.float32),
        lax.psum_scatter(
            g_a_out.astype(jnp.bfloat16), "ctx", scatter_dimension=1, tiled=True
        ).astype(jnp.float32),
        lax.psum_scatter(
            g_b_gu.astype(jnp.bfloat16), "ctx", scatter_dimension=0, tiled=True
        ).astype(jnp.float32),
        lax.psum_scatter(
            g_a_dn.astype(jnp.bfloat16), "ctx", scatter_dimension=1, tiled=True
        ).astype(jnp.float32),
        lax.psum_scatter(
            g_shared.astype(jnp.bfloat16), "ctx", scatter_dimension=0, tiled=True
        ).astype(jnp.float32),
        lax.psum_scatter(
            g_a_sh.astype(jnp.bfloat16), "ctx", scatter_dimension=0, tiled=True
        ).astype(jnp.float32),
        lax.psum_scatter(
            g_b_sh.astype(jnp.bfloat16), "ctx", scatter_dimension=0, tiled=True
        ).astype(jnp.float32),
    )
    out_shared, out_a_sh, out_b_sh = (reduced[10], reduced[11], reduced[12])
    out_a_in, out_a_gu, out_b_out, out_b_dn = (
        lax.psum_scatter(g_a_in, ("ctx", "tp"), scatter_dimension=0, tiled=True),
        lax.psum_scatter(g_a_gu, ("ctx", "tp"), scatter_dimension=0, tiled=True),
        lax.psum_scatter(g_b_out, ("ctx", "tp"), scatter_dimension=1, tiled=True),
        lax.psum_scatter(g_b_dn, ("ctx", "tp"), scatter_dimension=1, tiled=True),
    )
    return (
        mixed,
        input_grad,
        reduced[0],
        reduced[1],
        out_shared,
        reduced[2],
        grad_head,
        reduced[3],
        reduced[4],
        reduced[5],
        out_a_in,
        reduced[6],
        out_a_sh,
        out_b_sh,
        reduced[7],
        out_b_out,
        out_a_gu,
        reduced[8],
        reduced[9],
        out_b_dn,
    )


def solution(mesh):
    placed = (
        P("ctx", None),
        P(),
        P(None, "tp", None),
        P(),
        P(None, "tp"),
        P(None, "tp"),
        P("tp", None, None),
        P(None, None, "tp"),
        P("tp", None),
        P(),
        P(None, "tp", None),
        P(),
        P(),
        P("tp", None, None),
        P(),
        P(),
        P(None, None, "tp"),
        P("tp", None),
        P(),
        P(),
        P(),
        P("ctx", None),
    )
    return jax.shard_map(
        body,
        mesh=mesh,
        in_specs=placed,
        out_specs=(
            P("ctx", None),
            P("ctx", None),
            P(None, "ctx"),
            P("ctx", "tp", None),
            P("ctx", None),
            P("ctx", "tp"),
            P(None, "tp"),
            P("tp", None, "ctx"),
            P("ctx", None, "tp"),
            P("tp", "ctx"),
            P(("ctx", "tp"), None),
            P("ctx", "tp", None),
            P("ctx", None),
            P("ctx", None),
            P("tp", "ctx", None),
            P(None, ("ctx", "tp")),
            P(("ctx", "tp"), None),
            P("ctx", None, "tp"),
            P("tp", "ctx"),
            P(None, ("ctx", "tp")),
        ),
        check_vma=False,
    )
```

profile of v0, /device:TPU:0, one launch (start us, length us, event | category | flops | bytes accessed | tf_op | source)
XLA Modules:
  0.0 4013.3 jit_solution(17328026946815553553)
XLA Ops:
  47.7 21.5 all-gather.2
  92.5 24.8 all-gather.10.cloned.1.call-done
  127.5 39.7 all-gather.12.cloned.1.call-done
  167.2 33.5 while.47
  226.5 56.1 %all-reduce.26.cloned.1.call-done = bf16[512,2048]{1,0:T(8,128)(2,1)} async-done(((bf16[512,2048]{1,0:T(8,128)(2,1)}), bf16[512,2048]{1,0:T(8,128)(2,1)}) %all-reduce.26.cloned.1.call-update) | async-done | bytes 2097168 | tf_op jit(solution)/shard_map/psum | solution.py:256
  307.7 58.3 %all-reduce.28.cloned.1.call-done = bf16[512,2048]{1,0:T(8,128)(2,1)} async-done(((bf16[512,2048]{1,0:T(8,128)(2,1)}), bf16[512,2048]{1,0:T(8,128)(2,1)}) %all-reduce.28.cloned.1.call-update) | async-done | bytes 2097168 | tf_op jit(solution)/shard_map/psum | solution.py:284
  385.3 114.0 %while.49 = (s32[]{:T(128)}, f32[1,512,128]{2,1,0:T(8,128)S(1)}, bf16[16,512,128]{2,1,0:T(8,128)(2,1)}, bf16[16,512,128]{2,1,0:T(8,128)(2,1)}, s32[16]{0:T(128)S...) while((s32[]{:T(128)}, f32[1,512,128]{2,1,0:T(8,128)S(1)}, ...), condition=%wide.region_23.24_spmd.clone, body=%wide.region_21.23_spmd.clone.sunk | while | flops 338369024 | bytes 6705395 | solution.py:359
  543.7 33.9 while.48
  620.9 29.5 reduce-scatter.26.cloned.1.call-done
  681.1 48.5 %all-reduce.32.cloned.1.call-done = (bf16[512,2048]{1,0:T(8,128)(2,1)}, bf16[512,1024]{1,0:T(8,128)(2,1)}, bf16[512,2048]{1,0:T(8,128)(2,1)}) async-done(((bf16[512,2048]{1,0:T(8,128)(2,1)}, bf16[512,1024]{1,0:T(8,128)(2,1)}, bf16[512,2048]{1,0:T(8,128)(2,1)}), (bf16[512,2048]{1,0:T(8,128)(2,1)}, bf16[512,1024]{1,0:T(8,128)(2,1)}, bf16[512,2048]{1,0:T(8,128)(2,1)})) %all-reduce.32.cloned.1.call-update) | async-done | bytes 5242896 | tf_op jit(solution)/shard_map/psum | solution.py:269
  758.1 11.2 copy.202
  806.3 76.0 %reduce-scatter.50.cloned.1.call-done = bf16[128,512]{1,0:T(8,128)(2,1)} async-done(((bf16[2048,512]{1,0:T(8,128)(2,1)}), bf16[128,512]{1,0:T(8,128)(2,1)}) %reduce-scatter.50.cloned.1.call-update) | async-done | bytes 131088
  884.1 75.0 %reduce-scatter.48.cloned.1.call-done = bf16[128,512]{1,0:T(8,128)(2,1)} async-done(((bf16[2048,512]{1,0:T(8,128)(2,1)}), bf16[128,512]{1,0:T(8,128)(2,1)}) %reduce-scatter.48.cloned.1.call-update) | async-done | bytes 131088
  964.5 38.7 psum.47
  1003.2 31.4 reduce-scatter.46.cloned.1.call-done
  1045.2 64.6 %reduce-scatter.44.cloned.1.call-done = bf16[128,2]{1,0:T(8,128)(2,1)} async-done(((bf16[2048,2]{1,0:T(8,128)(2,1)}), bf16[128,2]{1,0:T(8,128)(2,1)}) %reduce-scatter.44.cloned.1.call-update) | async-done | bytes 528
  1111.2 73.5 %reduce-scatter.34.cloned.1.call-done = bf16[128,128]{1,0:T(8,128)(2,1)} async-done(((bf16[2048,128]{1,0:T(8,128)(2,1)}), bf16[128,128]{1,0:T(8,128)(2,1)}) %reduce-scatter.34.cloned.1.call-update) | async-done | bytes 32784 | tf_op jit(solution)/shard_map/reduce_scatter | solution.py:467
  1186.2 77.6 %reduce-scatter.28.cloned.1.call-done = bf16[128,1,896]{2,0,1:T(8,128)(2,1)} async-done(((bf16[2048,1,896]{2,0,1:T(8,128)(2,1)}), bf16[128,1,896]{2,0,1:T(8,128)(2,1)}) %reduce-scatter.28.cloned.1.call-update) | async-done | bytes 229392 | tf_op jit(solution)/shard_map/reduce_scatter | solution.py:437
  1265.8 113.2 %all-reduce.30.cloned.1.call-done = (bf16[2048,2,512]{2,1,0:T(2,128)(2,1)}, bf16[128,1,896]{2,0,1:T(8,128)(2,1)}, bf16[128,1024]{1,0:T(8,128)(2,1)}, bf16[128,2,512]{2,1,0:T(2,128)(2,1)}, bf16[512,128]{0,1:T(8,128)(2,1)}) async-done(((bf16[2048,2,512]{2,1,0:T(2,128)(2,1)}, bf16[128,1,896]{2,0,1:T(8,128)(2,1)}, bf16[128,1024]{1,0:T(8,128)(2,1)}, bf16[128,2,512]{2,1,0:T(2,128)(2,1)}, ...) | async-done | bytes 5079056
  1386.3 73.3 %reduce-scatter.30.cloned.1.call-done = bf16[128,1024]{1,0:T(8,128)(2,1)} async-done(((bf16[2048,1024]{1,0:T(8,128)(2,1)}), bf16[128,1024]{1,0:T(8,128)(2,1)}) %reduce-scatter.30.cloned.1.call-update) | async-done | bytes 262160 | tf_op jit(solution)/shard_map/reduce_scatter | solution.py:464
  1461.4 639.9 %reduce-scatter.40.cloned.1.call-done = f32[16,128]{1,0:T(8,128)} async-done(((f32[2048,128]{1,0:T(8,128)}), f32[16,128]{1,0:T(8,128)}) %reduce-scatter.40.cloned.1.call-update) | async-done | bytes 8208 | tf_op jit(solution)/shard_map/reduce_scatter | solution.py:477
  2101.3 635.4 %reduce-scatter.42.cloned.1.call-done = f32[128,16]{0,1:T(8,128)} async-done(((f32[128,2048]{0,1:T(8,128)}), f32[128,16]{0,1:T(8,128)}) %reduce-scatter.42.cloned.1.call-update) | async-done | bytes 8208 | tf_op jit(solution)/shard_map/reduce_scatter | solution.py:479
  2736.7 633.9 %reduce-scatter.38.cloned.1.call-done = f32[128,16]{0,1:T(8,128)} async-done(((f32[128,2048]{0,1:T(8,128)}), f32[128,16]{0,1:T(8,128)}) %reduce-scatter.38.cloned.1.call-update) | async-done | bytes 8208 | tf_op jit(solution)/shard_map/reduce_scatter | solution.py:478
  3370.6 635.6 %reduce-scatter.32.cloned.1.call-done = f32[16,128]{1,0:T(8,128)} async-done(((f32[2048,128]{1,0:T(8,128)}), f32[16,128]{1,0:T(8,128)}) %reduce-scatter.32.cloned.1.call-update) | async-done | bytes 8208 | tf_op jit(solution)/shard_map/reduce_scatter | solution.py:476
  (809 shorter events, 523.3 us)
Async XLA Ops:
  7.2 66.9 %all-gather.8.cloned.1.call-start = ((), (), s32[]{:S(2)}) async-start(), calls=%async_computation.14 | async-start | bytes 2228224 | tf_op jit(solution)/shard_map/all_gather | solution.py:230
  22.9 94.4 %all-gather.10.cloned.1.call-start = ((), (), s32[]{:S(2)}) async-start(), calls=%async_computation.15 | async-start | bytes 2228224 | tf_op jit(solution)/shard_map/all_gather | solution.py:231
  23.6 143.6 %all-gather.12.cloned.1.call-start = ((), (), s32[]{:S(2)}) async-start(), calls=%async_computation.28 | async-start | bytes 3342336 | tf_op jit(solution)/shard_map/all_gather | solution.py:20
  46.1 236.5 %all-reduce.26.cloned.1.call-start = ((), (), s32[]{:S(2)}) async-start(), calls=%async_computation.16 | async-start | bytes 4194304 | tf_op jit(solution)/shard_map/psum | solution.py:256
  217.6 148.4 %all-reduce.28.cloned.1.call-start = ((), (), s32[]{:S(2)}) async-start(), calls=%async_computation.17 | async-start | bytes 4194304 | tf_op jit(solution)/shard_map/psum | solution.py:284
  300.5 243.2 %all-gather.14.cloned.1.call-start = ((), (), s32[]{:S(2)}) async-start(), calls=%async_computation.29 | async-start | bytes 3342336 | tf_op jit(solution)/shard_map/all_gather | solution.py:43
  384.1 226.7 %reduce-scatter.24.cloned.1.call-start = ((), (), s32[]{:S(2)}) async-start(), calls=%async_computation.18 | async-start | bytes 2228224 | tf_op jit(solution)/shard_map/reduce_scatter | solution.py:369
  499.4 151.0 %reduce-scatter.26.cloned.1.call-start = ((), (), s32[]{:S(2)}) async-start(), calls=%async_computation.19 | async-start | bytes 2228224 | tf_op jit(solution)/shard_map/reduce_scatter | solution.py:375
  543.6 186.0 %all-reduce.32.cloned.1.call-start = ((), (), s32[]{:S(2)}) async-start(), calls=%async_computation.35 | async-start | bytes 10485760 | tf_op jit(solution)/shard_map/psum | solution.py:269
  652.0 153.1 %reduce-scatter.36.cloned.1.call-start = ((), (), s32[]{:S(2)}) async-start(), calls=%async_computation.24 | async-start | bytes 139264 | tf_op jit(solution)/shard_map/reduce_scatter | solution.py:455
  654.2 228.2 %reduce-scatter.50.cloned.1.call-start = ((), (), s32[]{:S(2)}) async-start(), calls=%async_computation.33 | async-start | bytes 2228224
  660.9 298.1 %reduce-scatter.48.cloned.1.call-start = ((), (), s32[]{:S(2)}) async-start(), calls=%async_computation.32 | async-start | bytes 2228224
  678.8 355.8 %reduce-scatter.46.cloned.1.call-start = ((), (), s32[]{:S(2)}) async-start(), calls=%async_computation.31 | async-start | bytes 557056
  680.6 429.2 %reduce-scatter.44.cloned.1.call-start = ((), (), s32[]{:S(2)}) async-start(), calls=%async_computation.30 | async-start | bytes 557056
  742.0 442.8 %reduce-scatter.34.cloned.1.call-start = ((), (), s32[]{:S(2)}) async-start(), calls=%async_computation.23 | async-start | bytes 557056 | tf_op jit(solution)/shard_map/reduce_scatter | solution.py:467
  746.3 517.5 %reduce-scatter.28.cloned.1.call-start = ((), (), s32[]{:S(2)}) async-start(), calls=%async_computation.20 | async-start | bytes 3899392 | tf_op jit(solution)/shard_map/reduce_scatter | solution.py:437
  751.6 627.4 %all-reduce.30.cloned.1.call-start = ((), (), s32[]{:S(2)}) async-start(), calls=%async_computation.34 | async-start | bytes 10158080
  779.6 680.0 %reduce-scatter.30.cloned.1.call-start = ((), (), s32[]{:S(2)}) async-start(), calls=%async_computation.21 | async-start | bytes 4456448 | tf_op jit(solution)/shard_map/reduce_scatter | solution.py:464
  784.1 1317.2 %reduce-scatter.40.cloned.1.call-start = ((), (), s32[]{:S(2)}) async-start(), calls=%async_computation.26 | async-start | bytes 1056768 | tf_op jit(solution)/shard_map/reduce_scatter | solution.py:477
  789.4 1947.3 %reduce-scatter.42.cloned.1.call-start = ((), (), s32[]{:S(2)}) async-start(), calls=%async_computation.27 | async-start | bytes 1056768 | tf_op jit(solution)/shard_map/reduce_scatter | solution.py:479
  793.8 2576.9 %reduce-scatter.38.cloned.1.call-start = ((), (), s32[]{:S(2)}) async-start(), calls=%async_computation.25 | async-start | bytes 1056768 | tf_op jit(solution)/shard_map/reduce_scatter | solution.py:478
  798.4 237.7 %copy-start.102 = (f32[512]{0:T(512)S(1)}, f32[512]{0:T(512)}, u32[]{:S(2)}) copy-start(f32[512]{0:T(512)} %copy-done.101) | copy-start | bytes 6148
  798.5 3207.8 %reduce-scatter.32.cloned.1.call-start = ((), (), s32[]{:S(2)}) async-start(), calls=%async_computation.22 | async-start | bytes 1056768 | tf_op jit(solution)/shard_map/reduce_scatter | solution.py:476
  1036.1 2970.1 %copy-start.1 = (bf16[1,512,2048]{2,1,0:T(8,128)(2,1)S(1)}, bf16[1,512,2048]{2,1,0:T(8,128)(2,1)}, u32[]{:S(2)}) copy-start(bf16[1,512,2048]{2,1,0:T(8,128)(2,1)} %param.34) | copy-start | bytes 6291460
  (144 other events, 3402.7 us)
Sparse Core Ops, SparseCore 0:
  23.0 47.5 all-gather.7
  73.3 43.9 all-gather.9
  120.0 47.1 all-gather.11
  217.7 64.8 all-reduce.25
  300.6 65.3 all-reduce.27
  384.2 47.2 all-gather.13
  499.5 73.6 reduce-scatter.23
  576.8 73.4 reduce-scatter.25
  653.0 76.6 all-reduce.31
  733.2 71.7 reduce-scatter.35
  808.6 73.6 reduce-scatter.49
  885.5 73.5 reduce-scatter.47
  963.1 71.4 reduce-scatter.45
  1038.3 71.5 reduce-scatter.43
  1113.2 71.5 reduce-scatter.33
  1188.0 75.7 reduce-scatter.27
  1267.6 111.3 all-reduce.29
  1382.2 77.3 reduce-scatter.29
  1462.6 638.5 reduce-scatter.39
  2104.0 632.6 reduce-scatter.41
  2739.7 630.8 reduce-scatter.37
  3373.5 632.6 reduce-scatter.31
where the time goes:
time: 4020 us; the launch traced here: 4010 us
  waiting for transfers between devices  3390 us (84%)
  matrix products  272 us (7%)
  other arithmetic  130 us (3%)
  local copies, waits for them, and re-layouts  125 us (3%)
  blocking collectives  60.2 us (1%)
    reduce_scatter x1, waiting for transfers between devices, body(): lax.psum_scatter(g_a_gu, ('ctx', 'tp'), scatter_dimension=0, tiled=True)  640 us
    reduce_scatter x1, waiting for transfers between devices, body(): lax.psum_scatter(g_a_in, ('ctx', 'tp'), scatter_dimension=0, tiled=True)  636 us
    reduce_scatter x1, waiting for transfers between devices, body(): lax.psum_scatter(g_b_dn, ('ctx', 'tp'), scatter_dimension=1, tiled=True)  635 us
    reduce_scatter x1, waiting for transfers between devices, body(): lax.psum_scatter(g_b_out, ('ctx', 'tp'), scatter_dimension=1, tiled=True)  634 us
    unnamed x27, waiting for transfers between devices  361 us
  transfers between devices with their start and end apart: 22, of which 19 were waited for; matrix products, arithmetic and copies ran while one was open for 10% of the time, Pallas kernels for 0%

commit v1 on v0

v1 whole, which is shorter than its diff:
```python
import functools

import jax
import jax.numpy as jnp
from jax import lax
from jax.experimental import pallas as pl
from jax.experimental.pallas import tpu as pltpu
from jax.sharding import PartitionSpec as P

MHEAD = 64
STATE = 256
QHEADS = 8
KVH = 2
HD = 128
RANK = 16
NORM_EPSILON = 1e-06

MESH = pl.DeviceIdType.MESH
VM = pl.BlockSpec(memory_space=pltpu.VMEM)
SM = pl.BlockSpec(memory_space=pltpu.SMEM)
BF = jnp.bfloat16
F32 = jnp.float32
DMA = pltpu.SemaphoreType.DMA
OFFSETS = (2, 1, 3)


def call(kernel, outs, ins, scratch, cid, name):
    return pl.pallas_call(
        kernel,
        out_shape=[jax.ShapeDtypeStruct(s, d) for s, d in outs],
        in_specs=[VM] * len(ins),
        out_specs=[VM] * len(outs),
        scratch_shapes=scratch,
        compiler_params=pltpu.CompilerParams(
            collective_id=cid, has_side_effects=True, vmem_limit_bytes=56 << 20
        ),
        name=name,
    )(*ins)


def greet(peers):
    barrier = pltpu.get_barrier_semaphore()
    for peer in peers:
        pl.semaphore_signal(barrier, inc=1, device_id=peer, device_id_type=MESH)
    pl.semaphore_wait(barrier, len(peers))


def send(src, dst, sems, slot, peer):
    cp = pltpu.make_async_remote_copy(
        src_ref=src,
        dst_ref=dst,
        send_sem=sems[0].at[slot],
        recv_sem=sems[1].at[slot],
        device_id=peer,
        device_id_type=MESH,
    )
    cp.start()
    return cp


def pair(*shape):
    return [DMA(shape), DMA(shape)]


def tp_place():
    ctx = lax.axis_index("ctx")
    tp = lax.axis_index("tp")
    return ctx, tp, tp // 2, tp % 2


def tp_peers(ctx, tp, z, c):
    return [(ctx, ((z + d) % 4) * 2 + c) for d in (1, 2, 3)] + [(ctx, z * 2 + 1 - c)]


def reduce_bufs(rows, width):
    return [
        pltpu.VMEM((4, rows, width), BF),
        pltpu.VMEM((3, rows, width), BF),
        pltpu.VMEM((3, rows, width), BF),
        *pair(4),
        *pair(3),
    ]


def reduce_start(part, bufs, place):
    sib, snd, rcv, s1s, s1r, s2s, s2r = bufs
    ctx, tp, z, c = place
    mate = (ctx, z * 2 + 1 - c)
    return [
        send(part.at[((z + off) % 4) * 2 + 1 - c], sib.at[k], (s1s, s1r), k, mate)
        for k, off in enumerate(OFFSETS + (0,))
    ]


def reduce_middle(part, bufs, place, first):
    sib, snd, rcv, s1s, s1r, s2s, s2r = bufs
    ctx, tp, z, c = place
    second = []
    for k, off in enumerate(OFFSETS):
        to = ((z + off) % 4) * 2 + c
        first[k].wait_recv()
        snd[k] = (part[to].astype(F32) + sib[k].astype(F32)).astype(BF)
        second.append(send(snd.at[k], rcv.at[k], (s2s, s2r), k, (ctx, to)))
    return second


def reduce_end(part, bufs, place, first, second):
    sib, snd, rcv = bufs[:3]
    first[3].wait_recv()
    total = part[place[1]].astype(F32) + sib[3].astype(F32)
    for k in range(3):
        second[k].wait_recv()
        total = total + rcv[k].astype(F32)
    for cp in first + second:
        cp.wait_send()
    return total


def share_sems():
    return [*pair(3), *pair(4)]


def share_start(out, sems, place):
    ctx, tp, z, c = place
    copies = [
        send(out.at[tp], out.at[tp], sems[:2], k, (ctx, ((z + off) % 4) * 2 + c))
        for k, off in enumerate(OFFSETS)
    ]
    return copies, send(out.at[tp], out.at[tp], sems[2:], 3, (ctx, z * 2 + 1 - c))


def share_end(out, sems, place, started):
    ctx, tp, z, c = place
    copies, own = started
    passed = [own]
    for k, off in sorted(enumerate(OFFSETS), key=lambda t: t[1] == 2):
        copies[k].wait_recv()
        at = ((z + 4 - off) % 4) * 2 + c
        passed.append(send(out.at[at], out.at[at], sems[2:], k, (ctx, z * 2 + 1 - c)))
    for cp in passed:
        cp.wait_recv()
    for cp in copies + passed:
        cp.wait_send()


def norm_scale(v):
    return lax.rsqrt(jnp.mean(v * v, axis=-1, keepdims=True) + NORM_EPSILON)


def norm_back(v, gain, grad):
    r = norm_scale(v)
    pulled = grad * gain
    inner = jnp.mean(pulled * v, axis=-1, keepdims=True)
    grad_v = r * pulled - v * (r * r * r) * inner
    return grad_v, jnp.sum(grad * v * r, axis=0, keepdims=True)


def dot(a, b):
    return jnp.dot(a, b, preferred_element_type=F32)


def dot_nt(a, b):
    return lax.dot_general(a, b, (((1,), (1,)), ((), ())), preferred_element_type=F32)


def dot_tn(a, b):
    return lax.dot_general(a, b, (((0,), (0,)), ((), ())), preferred_element_type=F32)


def mixer_kernel(part, source, gain, b_out, out, resid, *scratch):
    width = source.shape[1]
    place = tp_place()
    greet(tp_peers(*place))
    bufs, sems = scratch[:7], scratch[7:]
    first = reduce_start(part, bufs, place)
    total = reduce_end(part, bufs, place, first, reduce_middle(part, bufs, place, first))
    low = total[:, width:].astype(BF)
    residual = source[...].astype(F32) + total[:, :width] + dot(low, b_out[...])
    resid[...] = residual
    normed = residual * norm_scale(residual) * gain[...]
    out[place[1], :, :width] = normed.astype(BF)
    out[place[1], :, width:] = low
    share_end(out, sems, place, share_start(out, sems, place))


def mixer_exchange(part, source, gain, b_out):
    _, rows, wide = part.shape
    return call(
        mixer_kernel,
        [(part.shape, BF), (source.shape, F32)],
        [part, source, gain, b_out],
        reduce_bufs(rows, wide) + share_sems(),
        1,
        "mixer_exchange",
    )


def mlp_kernel(part, resid, gain, out_grad, b_dn, a_gu, mask, out, grad_resid, gain_part, *scratch):
    width = resid.shape[1]
    rank = a_gu.shape[1]
    wide = width + rank
    place = tp_place()
    tp = place[1]
    greet(tp_peers(*place))
    bufs, sems = scratch[:7], scratch[7:]
    first = reduce_start(part, bufs, place)
    total = reduce_end(part, bufs, place, first, reduce_middle(part, bufs, place, first))
    low_gu = (total[:, width:wide] * mask[...]).astype(BF)
    low_dn = total[:, wide + width :].astype(BF)
    residual = resid[...]
    grad = total[:, :width] + dot_nt(low_gu, a_gu[...])
    grad_v, grad_gain = norm_back(residual, gain[...], grad)
    grad_r = out_grad[...].astype(F32) + grad_v
    grad_resid[...] = grad_r
    gain_part[...] = grad_gain
    mixed = residual + total[:, wide : wide + width] + dot(low_dn, b_dn[...])
    out[tp, :, :width] = grad_r.astype(BF)
    out[tp, :, width:wide] = low_gu
    out[tp, :, wide : wide + width] = mixed.astype(BF)
    out[tp, :, wide + width :] = low_dn
    share_end(out, sems, place, share_start(out, sems, place))


def mlp_exchange(part, resid, gain, out_grad, b_dn, a_gu, mask):
    _, rows, wide = part.shape
    return call(
        mlp_kernel,
        [(part.shape, BF), (resid.shape, F32), (gain.shape, F32)],
        [part, resid, gain, out_grad, b_dn, a_gu, mask],
        reduce_bufs(rows, wide) + share_sems(),
        2,
        "mlp_exchange",
    )


def input_kernel(
    part, part_two, source, gain, grad_resid, a_in, a_sh, mask, gain_two, out, gains, two, *scratch
):
    width = source.shape[1]
    rank = a_in.shape[1]
    place = tp_place()
    tp = place[1]
    greet(tp_peers(*place))
    bufs, more, sems, sems_g = scratch[:7], scratch[7:14], scratch[14:18], scratch[18:]
    first = reduce_start(part, bufs, place)
    first_two = reduce_start(part_two, more, place)
    second = reduce_middle(part, bufs, place, first)
    second_two = reduce_middle(part_two, more, place, first_two)
    total = reduce_end(part, bufs, place, first, second)
    low_in = (total[:, width : width + rank] * mask[...]).astype(BF)
    low_sh = (total[:, width + rank :] * mask[...]).astype(BF)
    grad = total[:, :width] + dot_nt(low_in, a_in[...]) + dot_nt(low_sh, a_sh[...])
    grad_v, grad_gain = norm_back(source[...].astype(F32), gain[...], grad)
    out[tp, :, :width] = (grad_resid[...] + grad_v).astype(BF)
    out[tp, :, width : width + rank] = low_in
    out[tp, :, width + rank :] = low_sh
    gains[tp, 0:1] = grad_gain
    gains[tp, 1:2] = gain_two[...]
    gains[tp, 2:8] = jnp.zeros((6, width), F32)
    started = share_start(out, sems, place)
    started_g = share_start(gains, sems_g, place)
    two[...] = reduce_end(part_two, more, place, first_two, second_two).astype(BF)
    share_end(out, sems, place, started)
    share_end(gains, sems_g, place, started_g)


def input_exchange(part, part_two, source, gain, grad_resid, a_in, a_sh, mask, gain_two):
    _, rows, wide = part.shape
    _, tall, cols = part_two.shape
    return call(
        input_kernel,
        [(part.shape, BF), ((8, 8, source.shape[1]), F32), ((tall, cols), BF)],
        [part, part_two, source, gain, grad_resid, a_in, a_sh, mask, gain_two],
        reduce_bufs(rows, wide) + reduce_bufs(tall, cols) + share_sems() + share_sems(),
        3,
        "input_exchange",
    )


def ctx_place():
    ctx = lax.axis_index("ctx")
    return ctx, lax.axis_index("tp"), ctx // 4, ctx % 4


def spot(h, fast, slow):
    return slow * 4 + fast if h == 0 else fast * 4 + slow


def scatter_bufs(rows, width):
    most = max(rows - rows // 32 * 16, rows // 32 * 16)
    return [
        pltpu.VMEM((2, 3, most, width), BF),
        pltpu.VMEM((2, 3, 4, most, width), BF),
        pltpu.VMEM((2, 3, most, width), BF),
        *pair(2, 3, 4),
        *pair(2, 3),
    ]


def spans_of(rows):
    half = rows // 32 * 16
    return ((0, half), (half, rows - half))


def scatter_start(part, bufs, place):
    mid, r1, r2, s1s, s1r, s2s, s2r = bufs
    ctx, tp, y, x = place
    spans = spans_of(part.shape[1])
    first = {}
    for j in OFFSETS + (0,):
        for off in OFFSETS:
            for h in (0, 1):
                fast, slow = ((x, y), (y, x))[h]
                lo, size = spans[h]
                to = (fast + off) % 4
                first[h, off, j] = send(
                    part.at[spot(h, to, (slow + j) % 4), pl.ds(lo, size)],
                    r1.at[h, off - 1, j, pl.ds(0, size)],
                    (s1s, s1r),
                    (h, off - 1, j),
                    (spot(h, to, slow), tp),
                )
    return first


def scatter_middle(part, out, bufs, place, first):
    mid, r1, r2, s1s, s1r, s2s, s2r = bufs
    ctx, tp, y, x = place
    spans = spans_of(part.shape[1])
    second = {}
    for j in OFFSETS + (0,):
        for h in (0, 1):
            fast, slow = ((x, y), (y, x))[h]
            lo, size = spans[h]
            for off in OFFSETS:
                first[h, off, j].wait_recv()
            total = part[spot(h, fast, (slow + j) % 4), pl.ds(lo, size)].astype(F32)
            for off in (1, 2, 3):
                total = total + r1[h, off - 1, j, pl.ds(0, size)].astype(F32)
            if j == 0:
                out[pl.ds(lo, size)] = total
            else:
                mid[h, j - 1, pl.ds(0, size)] = total.astype(BF)
                second[h, j] = send(
                    mid.at[h, j - 1, pl.ds(0, size)],
                    r2.at[h, j - 1, pl.ds(0, size)],
                    (s2s, s2r),
                    (h, j - 1),
                    (spot(h, fast, (slow + j) % 4), tp),
                )
    return second


def scatter_end(part, out, bufs, first, second):
    r2 = bufs[2]
    for h, (lo, size) in enumerate(spans_of(part.shape[1])):
        for j in OFFSETS:
            second[h, j].wait_recv()
        total = out[pl.ds(lo, size)]
        for j in (1, 2, 3):
            total = total + r2[h, j - 1, pl.ds(0, size)].astype(F32)
        out[pl.ds(lo, size)] = total
    for cp in list(first.values()) + list(second.values()):
        cp.wait_send()


def ctx_peers(ctx, tp):
    return [((ctx + d) % 16, tp) for d in range(1, 16)]


def swap_start(src, dst, sems, place):
    ctx, tp = place[:2]
    return [
        send(src.at[(ctx + d) % 16], dst.at[ctx], sems, d - 1, ((ctx + d) % 16, tp))
        for d in range(1, 16)
    ]


def prefix_into(order, got, ent):
    running = jnp.zeros(ent.shape[1:], F32)
    for i in order:
        ent[i] = running
        running = got[i, 0:16] + got[i, 16:17] * running


def front_kernel(msg, kv, entering, kv_all, got, ent, *sems):
    place = ctx_place()
    ctx, tp, y, x = place
    c = tp % 2
    mate = (ctx, tp + 1 - 2 * c)
    greet(ctx_peers(ctx, tp) + [mate])
    s_one, s_two, s_kv1, s_kv2, s_m1, s_m2 = [sems[2 * k : 2 * k + 2] for k in range(6)]
    one = swap_start(msg, got, s_one, place)
    half = kv.shape[0] // 2
    part = half // 2
    base = pl.multiple_of(c * half, half)
    span = [pl.ds(pl.multiple_of(base + h * part, part), part) for h in (0, 1)]
    kv1 = {}
    for off in OFFSETS:
        for h in (0, 1):
            fast, slow = ((x, y), (y, x))[h]
            kv1[h, off] = send(
                kv.at[span[h]],
                kv_all.at[ctx, span[h]],
                s_kv1,
                (h, off - 1),
                (spot(h, (fast + off) % 4, slow), tp),
            )
    kv_all[ctx] = kv[...]
    got[ctx] = msg[ctx]
    for cp in one:
        cp.wait_recv()
    prefix_into(range(16), got, ent)
    two = swap_start(ent, entering, s_two, place)
    entering[ctx] = ent[ctx]
    kv2, to_mate = {}, []
    for off in OFFSETS:
        for h in (0, 1):
            kv1[h, off].wait_recv()
    for h in (0, 1):
        fast, slow = ((x, y), (y, x))[h]
        for off in OFFSETS:
            for k in range(4):
                at = spot(h, k, slow)
                kv2[h, off, k] = send(
                    kv_all.at[at, span[h]],
                    kv_all.at[at, span[h]],
                    s_kv2,
                    (h, off - 1, k),
                    (spot(h, fast, (slow + off) % 4), tp),
                )
    for off in OFFSETS:
        for h in (0, 1):
            fast, slow = ((x, y), (y, x))[h]
            at = spot(h, (fast + 4 - off) % 4, slow)
            to_mate.append(
                send(kv_all.at[at, span[h]], kv_all.at[at, span[h]], s_m1, (h, off - 1), mate)
            )
    for off in OFFSETS:
        for h in (0, 1):
            fast, slow = ((x, y), (y, x))[h]
            for k in range(4):
                kv2[h, off, k].wait_recv()
                at = spot(h, k, (slow + 4 - off) % 4)
                to_mate.append(
                    send(
                        kv_all.at[at, span[h]], kv_all.at[at, span[h]], s_m2, (h, off - 1, k), mate
                    )
                )
    for cp in two + to_mate:
        cp.wait_recv()
    for cp in one + two + to_mate + list(kv1.values()) + list(kv2.values()):
        cp.wait_send()


def front_exchange(msg, kv):
    _, _, width = msg.shape
    return call(
        front_kernel,
        [((16, 16, width), F32), ((16,) + kv.shape, BF)],
        [msg, kv],
        [
            pltpu.VMEM(msg.shape, F32),
            pltpu.VMEM((16, 16, width), F32),
            *pair(15),
            *pair(15),
            *pair(2, 3),
            *pair(2, 3, 4),
            *pair(2, 3),
            *pair(2, 3, 4),
        ],
        4,
        "front_exchange",
    )


def back_kernel(msg, dkv, leaving, out, got, ent, mate_buf, both, *scratch):
    place = ctx_place()
    ctx, tp, y, x = place
    c = tp % 2
    mate = (ctx, tp + 1 - 2 * c)
    greet(ctx_peers(ctx, tp) + [mate])
    s_one, s_two, s_mate, bufs = scratch[0:2], scratch[2:4], scratch[4:6], scratch[6:]
    one = swap_start(msg, got, s_one, place)
    half = dkv.shape[1] // 2
    mine = pl.ds(pl.multiple_of(c * half, half), half)
    other = pl.ds(pl.multiple_of((1 - c) * half, half), half)
    cps = [
        send(
            dkv.at[pl.ds(4 * k, 4), other], mate_buf.at[pl.ds(4 * k, 4)], s_mate, k, mate
        )
        for k in range(4)
    ]
    got[ctx] = msg[ctx]
    for k in range(4):
        cps[k].wait_recv()
        for i in range(4 * k, 4 * k + 4):
            both[i] = (dkv[i, mine].astype(F32) + mate_buf[i].astype(F32)).astype(BF)
    first = scatter_start(both, bufs, place)
    for cp in one:
        cp.wait_recv()
    prefix_into(range(15, -1, -1), got, ent)
    two = swap_start(ent, leaving, s_two, place)
    leaving[ctx] = ent[ctx]
    second = scatter_middle(both, out, bufs, place, first)
    scatter_end(both, out, bufs, first, second)
    for cp in two:
        cp.wait_recv()
    for cp in one + two + cps:
        cp.wait_send()


def back_exchange(msg, dkv):
    _, _, width = msg.shape
    _, tall, cols = dkv.shape
    half = tall // 2
    return call(
        back_kernel,
        [((16, 16, width), F32), ((half, cols), F32)],
        [msg, dkv],
        [
            pltpu.VMEM(msg.shape, F32),
            pltpu.VMEM((16, 16, width), F32),
            pltpu.VMEM((16, half, cols), BF),
            pltpu.VMEM((16, half, cols), BF),
            *pair(15),
            *pair(15),
            *pair(4),
            *scatter_bufs(half, cols),
        ],
        5,
        "back_exchange",
    )


def tail_kernel(big, small, head, big_out, small_out, shared, head_out, heads, *scratch):
    place = ctx_place()
    ctx, tp = place[:2]
    tp_at = tp_place()
    greet(ctx_peers(ctx, tp) + tp_peers(*tp_at))
    bufs, more, s_head, sems = scratch[:7], scratch[7:14], scratch[14:16], scratch[16:]
    first_s = scatter_start(small, more, place)
    first = scatter_start(big, bufs, place)
    sent = [
        send(head, heads.at[ctx], s_head, d - 1, ((ctx + d) % 16, tp)) for d in range(1, 16)
    ]
    heads[ctx] = head[...]
    second_s = scatter_middle(small, small_out, more, place, first_s)
    second = scatter_middle(big, big_out, bufs, place, first)
    scatter_end(small, small_out, more, first_s, second_s)
    shared[tp] = small_out[pl.ds(0, shared.shape[1])]
    started = share_start(shared, sems, tp_at)
    scatter_end(big, big_out, bufs, first, second)
    for cp in sent:
        cp.wait_recv()
    head_out[...] = jnp.sum(heads[...], axis=0)
    share_end(shared, sems, tp_at, started)
    for cp in sent:
        cp.wait_send()


def tail_exchange(big, small, head, shared_rows):
    _, tall, wide = big.shape
    _, rows, cols = small.shape
    return call(
        tail_kernel,
        [
            ((tall, wide), F32),
            ((rows, cols), F32),
            ((8, shared_rows, cols), F32),
            (head.shape, F32),
        ],
        [big, small, head],
        [
            pltpu.VMEM((16,) + head.shape, F32),
            *scatter_bufs(tall, wide),
            *scatter_bufs(rows, cols),
            *pair(15),
            *share_sems(),
        ],
        6,
        "tail_exchange",
    )


def flash_kernel(scale, at, q_t, kv, start, out_t, lse):
    ctx = at[0]
    block, size = kv.shape[1], q_t.shape[1]
    queries = q_t[...]
    begin = start[...]

    def step(i, carry, diagonal):
        top, total, acc = carry
        s = dot(kv[i, :, :HD], queries)
        key = i * block + lax.broadcasted_iota(jnp.int32, s.shape, 0)
        allowed = key >= begin
        if diagonal:
            allowed &= key <= ctx * block + lax.broadcasted_iota(jnp.int32, s.shape, 1)
        s = jnp.where(allowed, s * scale, -1e30)
        new = jnp.maximum(top, jnp.max(s, axis=0, keepdims=True))
        p = jnp.where(allowed, jnp.exp(s - new), 0.0)
        fade = jnp.exp(top - new)
        total = total * fade + jnp.sum(p, axis=0, keepdims=True)
        acc = acc * fade + dot_tn(kv[i, :, HD:], p.astype(BF))
        return new, total, acc

    carry = (
        jnp.full((1, size), -1e30, F32),
        jnp.zeros((1, size), F32),
        jnp.zeros((HD, size), F32),
    )
    carry = lax.fori_loop(at[1], ctx, lambda i, k: step(i, k, False), carry)
    top, total, acc = step(ctx, carry, True)
    out_t[...] = acc / total
    lse[...] = top + jnp.log(total)


def plain_call(kernel, outs, ins, specs, name):
    return pl.pallas_call(
        kernel,
        out_shape=[jax.ShapeDtypeStruct(s, d) for s, d in outs],
        in_specs=specs,
        out_specs=[VM] * len(outs),
        compiler_params=pltpu.CompilerParams(vmem_limit_bytes=56 << 20),
        name=name,
    )(*ins)


def flash_forward(at, q_t, kv, start, scale):
    return plain_call(
        functools.partial(flash_kernel, scale),
        [(q_t.shape, F32), ((1, q_t.shape[1]), F32)],
        [at, q_t, kv, start],
        [SM, VM, VM, VM],
        "flash_forward",
    )


def flash_back_kernel(scale, at, q_t, q, kv, start, lse, grad_t, grad, delta, dq_t, dkv):
    ctx = at[0]
    block = kv.shape[1]
    dkv[...] = jnp.zeros(dkv.shape, BF)
    queries_t, queries = q_t[...], q[...]
    og_t, og = grad_t[...], grad[...]
    begin, offset, low = start[...], lse[...], delta[...]

    def step(i, acc, diagonal):
        keys = kv[i, :, :HD]
        s = dot(keys, queries_t)
        key = i * block + lax.broadcasted_iota(jnp.int32, s.shape, 0)
        allowed = key >= begin
        if diagonal:
            allowed &= key <= ctx * block + lax.broadcasted_iota(jnp.int32, s.shape, 1)
        p = jnp.exp(jnp.where(allowed, s * scale - offset, -1e30))
        dp = dot(kv[i, :, HD:], og_t)
        ds = (p * (dp - low)).astype(BF)
        dkv[i, :, :HD] = (dot(ds, queries) * scale).astype(BF)
        dkv[i, :, HD:] = dot(p.astype(BF), og).astype(BF)
        return acc + dot_tn(keys, ds)

    acc = jnp.zeros(q_t.shape, F32)
    acc = lax.fori_loop(at[1], ctx, lambda i, k: step(i, k, False), acc)
    dq_t[...] = step(ctx, acc, True) * scale


def flash_backward(at, q_t, q, kv, start, lse, grad_t, grad, delta, scale):
    return plain_call(
        functools.partial(flash_back_kernel, scale),
        [(q_t.shape, F32), (kv.shape, BF)],
        [at, q_t, q, kv, start, lse, grad_t, grad, delta],
        [SM] + [VM] * 8,
        "flash_backward",
    )


def soft_plus(values):
    return jnp.maximum(values, 0.0) + jnp.log1p(jnp.exp(-jnp.abs(values)))


def doc_index(positions, doc_lengths):
    bounds = jnp.cumsum(doc_lengths)
    return jnp.sum((positions[:, None] >= bounds[None, :]).astype(jnp.int32), axis=1)


def adapter_mask(doc_ids, adapter_ids, columns):
    seq_count = adapter_ids.shape[0]
    chosen = jnp.sum(
        jnp.where(doc_ids[:, None] == jnp.arange(seq_count)[None, :], adapter_ids[None, :], 0),
        axis=1,
    )
    return (chosen[:, None] == jnp.arange(columns)[None, :] // RANK).astype(F32)


def spread(per_head):
    return jnp.repeat(per_head, MHEAD, axis=1)


def by_head(flat):
    return flat.reshape(flat.shape[0], -1, MHEAD).transpose(1, 0, 2)


def flat_heads(split):
    return split.transpose(1, 0, 2).reshape(split.shape[1], -1)


def state_message(state, decay):
    wide = jnp.repeat(decay, MHEAD)
    rows = jnp.broadcast_to(wide[None, None, :], (16, 8, wide.shape[0]))
    return jnp.concatenate([state.reshape(16, 16, -1), rows], axis=1)


def body(
    hidden_in,
    norm_gains,
    w_in,
    w_shared,
    w_dt,
    head_params,
    w_out,
    w_gu,
    w_down,
    a_in,
    b_in,
    a_sh,
    b_sh,
    a_out,
    b_out,
    a_gu,
    b_gu,
    a_dn,
    b_dn,
    adapter_ids,
    doc_lengths,
    out_grad,
):
    rows, width = hidden_in.shape
    heads = head_params.shape[1]
    inner = heads * MHEAD
    tp_count = lax.axis_size("tp")
    share = rows // tp_count
    ctx_at = lax.axis_index("ctx")
    tp_at = lax.axis_index("tp")
    positions = ctx_at * rows + jnp.arange(rows, dtype=jnp.int32)
    doc_ids = doc_index(positions, doc_lengths)
    doc_before = doc_index(jnp.maximum(positions[:1] - 1, 0), doc_lengths)[0]
    bounds = jnp.cumsum(doc_lengths)
    starts = jnp.sum(
        jnp.where(doc_ids[:, None] == jnp.arange(1, 1 + bounds.shape[0])[None, :], bounds[None, :], 0),
        axis=1,
    )
    starts_row = starts[None, :]
    at = jnp.stack([ctx_at, jnp.min(starts) // rows]).astype(jnp.int32)
    mask = adapter_mask(doc_ids, adapter_ids, a_in.shape[1])

    def rows_of(array):
        return lax.dynamic_slice_in_dim(array, tp_at * share, share, 0)

    mask_rows = rows_of(mask)
    w_in = w_in.reshape(width, -1)
    b_in = b_in.reshape(b_in.shape[0], -1)
    w_out = w_out.reshape(-1, width)
    a_out = a_out.reshape(-1, a_out.shape[2])
    w_gu = w_gu.reshape(width, -1)
    b_gu = b_gu.reshape(b_gu.shape[0], -1)
    hidden = w_down.shape[0]
    rank = a_in.shape[1]
    scale = HD ** (-0.5)
    gain_one, gain_two = norm_gains[0:1], norm_gains[1:2]
    source = hidden_in.astype(F32)
    normed_one = (source * norm_scale(source) * gain_one).astype(BF)
    low_in = (dot(normed_one, a_in) * mask).astype(BF)
    h_one = (dot(normed_one, w_in) + dot(low_in, b_in)).astype(BF)
    low_sh = (dot(normed_one, a_sh) * mask).astype(BF)
    h_two = (dot(normed_one, w_shared) + dot(low_sh, b_sh)).astype(BF)
    dt_raw = dot(normed_one, w_dt)
    gate = h_one[:, :inner].astype(F32)
    xs = h_one[:, inner : 2 * inner]
    xs_f = xs.astype(F32)
    q = h_one[:, 2 * inner :]
    q_t = q.T
    bm, cm = h_two[:, :STATE], h_two[:, STATE : 2 * STATE]
    kv_group = tp_at // (QHEADS // KVH)
    key_col = 2 * STATE + kv_group * HD
    keys_mine = lax.dynamic_slice_in_dim(h_two, key_col, HD, 1)
    vals_mine = lax.dynamic_slice_in_dim(h_two, key_col + KVH * HD, HD, 1)

    pre = dt_raw + head_params[0]
    dt = soft_plus(pre)
    rate = jnp.exp(head_params[1])
    order = jnp.arange(rows)
    tri = (order[:, None] >= order[None, :]).astype(F32)
    decay = jnp.dot(tri, -dt * rate, precision=lax.Precision.HIGHEST)
    decay_t, dt_t = decay.T, dt.T
    allowed = (order[:, None] >= order[None, :]) & (doc_ids[:, None] == doc_ids[None, :])
    gap = jnp.where(allowed[None], decay_t[:, :, None] - decay_t[:, None, :], -1e30)
    fade = jnp.exp(gap)
    inter = dot_nt(cm, bm)
    pulls = inter[None] * fade
    mixing = (pulls * dt_t[:, None, :]).astype(BF)
    xs_h = by_head(xs)
    inner_y = flat_heads(
        lax.dot_general(mixing, xs_h, (((2,), (1,)), ((0,), (0,))), preferred_element_type=F32)
    )
    tail = jnp.where(
        (doc_ids == doc_ids[-1])[:, None], jnp.exp(decay[-1][None, :] - decay), 0.0
    )
    tail_dt = tail * dt
    state_out = dot_tn(bm, (spread(tail_dt) * xs_f).astype(BF))
    total_decay = jnp.exp(decay[-1]) * (doc_ids[-1] == doc_before).astype(F32)
    entering, kv_all = front_exchange(
        state_message(state_out, total_decay), jnp.concatenate([keys_mine, vals_mine], axis=1)
    )
    entering = entering.reshape(STATE, inner)
    entering_low = entering.astype(BF)
    reach = spread(jnp.exp(decay) * (doc_ids == doc_before).astype(F32)[:, None])
    cross = dot(cm, entering_low) * reach
    skip = jnp.repeat(head_params[2], MHEAD)[None, :]
    ssd = inner_y + cross + skip * xs_f
    gate_sig = jax.nn.sigmoid(gate)
    gated = ssd * (gate * gate_sig)

    attn_t, lse = flash_forward(at, q_t, kv_all, starts_row, scale)
    merged = jnp.concatenate([gated, attn_t.T], axis=1).astype(BF)
    low_out_part = dot(merged, a_out) * mask
    mix_part = jnp.concatenate([dot(merged, w_out).astype(BF), low_out_part.astype(BF)], axis=1)
    shared_mix, resid = mixer_exchange(
        mix_part.reshape(tp_count, share, -1), rows_of(hidden_in), gain_two, b_out
    )
    shared_mix = shared_mix.reshape(rows, -1)
    normed_two, low_out = shared_mix[:, :width], shared_mix[:, width:]

    low_gu = (dot(normed_two, a_gu) * mask).astype(BF)
    h_gu = (dot(normed_two, w_gu) + dot(low_gu, b_gu)).astype(BF).astype(F32)
    gate_mlp, up = h_gu[:, :hidden], h_gu[:, hidden:]
    sig = jax.nn.sigmoid(gate_mlp)
    act = (gate_mlp * sig * up).astype(BF)
    low_dn_part = dot(act, a_dn) * mask
    mlp_part = dot(act, w_down)
    grad_low_dn = (dot_nt(out_grad, b_dn) * mask).astype(BF)
    grad_act = (dot_nt(out_grad, w_down) + dot_nt(grad_low_dn, a_dn)).astype(BF).astype(F32)
    grad_gu = jnp.concatenate(
        [grad_act * up * sig * (1.0 + gate_mlp * (1.0 - sig)), grad_act * (gate_mlp * sig)], axis=1
    ).astype(BF)
    grad_low_gu_part = dot_nt(grad_gu, b_gu)
    grad_two_part = dot_nt(grad_gu, w_gu)
    g_gu = dot_tn(normed_two, grad_gu).astype(BF).reshape(16, -1, 2 * hidden)
    g_b_gu = dot_tn(low_gu, grad_gu).astype(BF).reshape(16, -1, 2 * hidden)
    g_dn = dot_tn(out_grad, act).astype(BF).reshape(16, -1, hidden)
    g_a_dn = dot_tn(grad_low_dn, act).astype(BF).reshape(16, -1, hidden)
    early = jnp.concatenate(
        [jnp.concatenate([g_gu, g_dn], axis=2), jnp.concatenate([g_b_gu, g_a_dn], axis=2)], axis=1
    )
    early_rows = early.shape[1]
    early = lax.psum_scatter(
        early.reshape(16 * early_rows, -1), "ctx", scatter_dimension=0, tiled=True
    )
    part = jnp.concatenate(
        [
            grad_two_part.astype(BF),
            grad_low_gu_part.astype(BF),
            mlp_part.astype(BF),
            low_dn_part.astype(BF),
        ],
        axis=1,
    )
    shared_mlp, grad_resid, gain_part_two = mlp_exchange(
        part.reshape(tp_count, share, -1), resid, gain_two, rows_of(out_grad), b_dn, a_gu, mask_rows
    )
    shared_mlp = shared_mlp.reshape(rows, -1)
    wide = width + rank
    grad_mixer, grad_low_gu = shared_mlp[:, :width], shared_mlp[:, width:wide]
    mixed, low_dn = shared_mlp[:, wide : wide + width], shared_mlp[:, wide + width :]

    grad_low_out = (dot_nt(grad_mixer, b_out) * mask).astype(BF)
    grad_merged = (dot_nt(grad_mixer, w_out) + dot_nt(grad_low_out, a_out)).astype(BF)
    late = dot_tn(grad_mixer, merged).astype(BF)
    late = lax.psum_scatter(late, "ctx", scatter_dimension=0, tiled=True)
    grad_gated = grad_merged[:, :inner].astype(F32)
    grad_attn = grad_merged[:, inner:]
    grad_ssd = grad_gated * (gate * gate_sig)
    grad_gate = grad_gated * ssd * gate_sig * (1.0 + gate * (1.0 - gate_sig))
    grad_attn_t = grad_attn.T
    delta = jnp.sum(grad_attn_t.astype(F32) * attn_t, axis=0, keepdims=True)
    dq_t, dkv = flash_backward(
        at, q_t, q, kv_all, starts_row, lse, grad_attn_t, grad_attn, delta, scale
    )
    dy = grad_ssd.astype(BF)
    dy_h = by_head(dy)
    reached = (reach * grad_ssd).astype(BF)
    pull_state = dot_tn(cm, reached)
    leaving, dkv_sum = back_exchange(state_message(pull_state, total_decay), dkv)
    leaving = leaving.reshape(STATE, inner)
    leaving_low = leaving.astype(BF)
    d_mix = lax.dot_general(dy_h, xs_h, (((2,), (2,)), ((0,), (0,))), preferred_element_type=F32)
    d_inter = jnp.sum(d_mix * (fade * dt_t[:, None, :]), axis=0).astype(BF)
    weighted = d_mix * pulls
    col = jnp.sum(weighted, axis=1).T
    row = jnp.sum(weighted * dt_t[:, None, :], axis=2).T
    dx_inner = flat_heads(
        lax.dot_general(mixing, dy_h, (((1,), (1,)), ((0,), (0,))), preferred_element_type=F32)
    )
    from_state = dot(bm, leaving_low)

    def head_sums(flat):
        return jnp.sum(flat.reshape(flat.shape[0], heads, MHEAD), axis=2)

    held = head_sums(from_state * xs_f) * tail
    d_cross = head_sums(cross * grad_ssd)
    d_decay = row - col * dt + d_cross - held * dt
    d_last = jnp.sum(held * dt, axis=0) + total_decay * head_sums(
        jnp.sum(leaving * entering, axis=0)[None]
    )[0]
    d_log = jnp.dot(tri.T, d_decay, precision=lax.Precision.HIGHEST) + d_last[None, :]
    grad_dt = (col + held - rate * d_log) * jax.nn.sigmoid(pre)
    grad_x = dx_inner + spread(tail_dt) * from_state + skip * grad_ssd
    grad_bm = dot_tn(d_inter, cm) + dot_nt((spread(tail_dt) * xs_f).astype(BF), leaving_low)
    grad_cm = dot(d_inter, bm) + dot_nt(reached, entering_low)
    grad_head = jnp.stack(
        [
            jnp.sum(grad_dt, axis=0),
            -jnp.sum(dt * rate * d_log, axis=0),
            jnp.sum(head_sums(grad_ssd * xs_f), axis=0),
        ]
    )
    grad_one = jnp.concatenate([grad_gate, grad_x, dq_t.T], axis=1).astype(BF)
    half = rows // 2
    dkv_rows = lax.dynamic_update_slice_in_dim(
        jnp.zeros((rows, 2 * HD), F32), dkv_sum, (tp_at % 2) * half, 0
    ).astype(BF)
    group = (jnp.arange(KVH) == kv_group).astype(BF)[None, :, None]
    grad_two = jnp.concatenate(
        [
            grad_bm.astype(BF),
            grad_cm.astype(BF),
            (dkv_rows[:, None, :HD] * group).reshape(rows, KVH * HD),
            (dkv_rows[:, None, HD:] * group).reshape(rows, KVH * HD),
        ],
        axis=1,
    )
    grad_dt_low = grad_dt.astype(BF)
    norm_part = dot_nt(grad_one, w_in) + dot_nt(grad_two, w_shared) + dot_nt(grad_dt_low, w_dt)
    part = jnp.concatenate(
        [
            norm_part.astype(BF),
            dot_nt(grad_one, b_in).astype(BF),
            dot_nt(grad_two, b_sh).astype(BF),
        ],
        axis=1,
    )
    two_blocks = grad_two.reshape(rows, tp_count, -1).transpose(1, 0, 2)
    shared_in, gains, two_mine = input_exchange(
        part.reshape(tp_count, share, -1),
        two_blocks,
        rows_of(hidden_in),
        gain_one,
        grad_resid,
        a_in,
        a_sh,
        mask_rows,
        gain_part_two,
    )
    shared_in = shared_in.reshape(rows, -1)
    input_grad = shared_in[:, :width].astype(F32)
    grad_low_in, grad_low_sh = shared_in[:, width:wide], shared_in[:, wide:]
    gain_sum = jnp.sum(gains, axis=0)

    pad_dt = jnp.concatenate(
        [grad_one, grad_dt_low, jnp.zeros((rows, 128 - heads), BF)], axis=1
    )
    g_in = dot_tn(normed_one, pad_dt).astype(BF).reshape(16, -1, pad_dt.shape[1])
    g_b_in = dot_tn(low_in, pad_dt).astype(BF).reshape(16, -1, pad_dt.shape[1])
    big = jnp.concatenate([g_in, g_b_in, jnp.zeros_like(g_b_in)], axis=1)

    def my_slice(full):
        cut = full.astype(BF).reshape(16, tp_count, -1, full.shape[1])
        return lax.dynamic_index_in_dim(cut, tp_at, 1, keepdims=False)

    def by_ctx(full):
        return full.astype(BF).reshape(16, -1, full.shape[1])

    gain_rows = gain_sum.astype(BF).reshape(8, 16, -1).transpose(1, 0, 2)
    small = jnp.concatenate(
        [
            by_ctx(dot_tn(normed_one, two_mine)),
            my_slice(dot_tn(normed_one, grad_low_sh)),
            by_ctx(dot_tn(low_sh, two_mine)),
            gain_rows,
            by_ctx(dot_tn(merged, grad_low_out)),
            my_slice(dot_tn(normed_one, grad_low_in)),
            my_slice(dot_tn(normed_two, grad_low_gu)),
            my_slice(dot_tn(grad_mixer, low_out)),
            my_slice(dot_tn(out_grad, low_dn)),
        ],
        axis=1,
    )
    head_tile = jnp.pad(grad_head, ((0, 5), (0, 128 - heads)))
    big_sum, small_sum, shared, head_sum = tail_exchange(big, small, head_tile, 152)
    deep = width // 16
    out_shared = shared[:, :deep].transpose(1, 0, 2).reshape(deep, -1)
    out_a_sh = shared[:, deep : deep + 16].reshape(deep, -1)
    out_b_sh = shared[:, deep + 16 : deep + 24].transpose(1, 0, 2).reshape(8, -1)
    spot_at = deep + 24
    out_gain = small_sum[spot_at : spot_at + 2]
    spot_at += 8
    out_a_out = small_sum[spot_at : spot_at + 32]
    spot_at += 32
    four = [small_sum[spot_at + 16 * k : spot_at + 16 * (k + 1)] for k in range(4)]
    early = early.astype(F32)
    return (
        mixed.astype(F32),
        input_grad,
        out_gain,
        big_sum[:deep, : w_in.shape[1]].reshape(deep, 1, -1),
        out_shared,
        big_sum[:deep, w_in.shape[1] : w_in.shape[1] + heads],
        head_sum[:3, :heads],
        late.astype(F32).T[None],
        early[:deep, : 2 * hidden].reshape(deep, 2, hidden),
        early[:deep, 2 * hidden :].T,
        four[0],
        big_sum[deep : deep + 8, : w_in.shape[1]].reshape(8, 1, -1),
        out_a_sh,
        out_b_sh,
        out_a_out[None],
        four[2].T,
        four[1],
        early[deep : deep + 8, : 2 * hidden].reshape(8, 2, hidden),
        early[deep : deep + 8, 2 * hidden :].T,
        four[3].T,
    )
def solution(mesh):
    placed = (
        P("ctx", None),
        P(),
        P(None, "tp", None),
        P(),
        P(None, "tp"),
        P(None, "tp"),
        P("tp", None, None),
        P(None, None, "tp"),
        P("tp", None),
        P(),
        P(None, "tp", None),
        P(),
        P(),
        P("tp", None, None),
        P(),
        P(),
        P(None, None, "tp"),
        P("tp", None),
        P(),
        P(),
        P(),
        P("ctx", None),
    )
    return jax.shard_map(
        body,
        mesh=mesh,
        in_specs=placed,
        out_specs=(
            P("ctx", None),
            P("ctx", None),
            P(None, "ctx"),
            P("ctx", "tp", None),
            P("ctx", None),
            P("ctx", "tp"),
            P(None, "tp"),
            P("tp", None, "ctx"),
            P("ctx", None, "tp"),
            P("tp", "ctx"),
            P(("ctx", "tp"), None),
            P("ctx", "tp", None),
            P("ctx", None),
            P("ctx", None),
            P("tp", "ctx", None),
            P(None, ("ctx", "tp")),
            P(("ctx", "tp"), None),
            P("ctx", None, "tp"),
            P("tp", "ctx"),
            P(None, ("ctx", "tp")),
        ),
        check_vma=False,
    )
```

time: 4020 us -> 601 us (0.15)
  waiting for transfers between devices: 3390 us -> 0.04 us
  Pallas kernels: 0 us -> 317 us
  matrix products: 272 us -> 115 us
  other arithmetic: 130 us -> 53.6 us
  blocking collectives: 60.2 us -> 0 us
    reduce_scatter x10 -> x1, waiting for transfers between devices: 2800 us -> 0.01 us  [body(): late = lax.psum_scatter(late, 'ctx', scatter_dimension=0, tiled=True)]
    unnamed x27 -> x3, waiting for transfers between devices: 361 us -> 0.03 us
    pallas_call x0 -> x8, Pallas kernels: none -> 317 us  [the longest x6 307 us: call(): pl.pallas_call(kernel, out_shape=[jax.ShapeDtypeStruct(s, d) for s, d in...]
    psum x3 -> x0, waiting for transfers between devices: 163 us -> none  [the longest x1 58.3 us: body(): lax.psum(grad_normed_two.astype(jnp.bfloat16), 'tp').astype(jnp.float32)]
    dot_general x146 -> x56, matrix products: 271 us -> 115 us  [the longest x17 35.2 us: dot(): return jnp.dot(a, b, preferred_element_type=F32)]
    all_gather x4 -> x0, waiting for transfers between devices: 64.5 us -> none  [the longest x1 39.7 us: prefix(): lax.all_gather(part.astype(kind), axis)]
    dynamic_slice x80 -> x1, local copies, waits for them, and re-layouts: 46.8 us -> 1.86 us  [rows_of(): return lax.dynamic_slice_in_dim(array, tp_at * share, share, 0)]
  transfers between devices with their start and end apart: 22 -> 2, of which waited for: 19 -> 0; matrix products, arithmetic and copies ran while one was open for 10% -> 23% of each run, Pallas kernels for 0% -> 28%
where the time goes in v1:
time: 601 us; the launch traced here: 594 us
  Pallas kernels  317 us (53%)
  matrix products  115 us (19%)
  local copies, waits for them, and re-layouts  87.5 us (15%)
  other arithmetic  53.6 us (9%)
  between operations  20.7 us (3%)
    pallas_call x6, Pallas kernels, call(): pl.pallas_call(kernel, out_shape=[jax.ShapeDtypeStruct(s, d) for s, d in...  307 us
    dot_general x17, matrix products, dot(): return jnp.dot(a, b, preferred_element_type=F32)  35.2 us
    dot_general x16, matrix products, dot_nt(): lax.dot_general(a, b, (((1,), (1,)), ((), ())), preferred_element_type=F32)  32.7 us
    dot_general x18, matrix products, dot_tn(): lax.dot_general(a, b, (((0,), (0,)), ((), ())), preferred_element_type=F32)  29.8 us
    unnamed x226, local copies, waits for them, and re-layouts  21.6 us
  transfers between devices with their start and end apart: 2, of which 0 were waited for; matrix products, arithmetic and copies ran while one was open for 23% of the time, Pallas kernels for 28%

profile of v1, /device:TPU:0, one launch (start us, length us, event | category | flops | bytes accessed | tf_op | source)
XLA Modules:
  0.0 593.8 jit_solution(3989515114636623271)
XLA Ops:
  25.9 5.1 fusion.8
  34.8 5.4 copy.329
  42.3 6.6 %fusion.129 = f32[512,1024]{1,0:T(8,128)} fusion(bf16[512,2048]{1,0:T(8,128)(2,1)} %copy-done.2, bf16[2048,1024]{1,0:T(8,128)(2,1)} %param.25), kind=kOutput, calls=%fused_computation.263 | convolution fusion | flops 2147483648 | bytes 8388608 | tf_op jit(solution)/shard_map/dot_general | solution.py:159
  59.5 39.6 %front_exchange.1 = (f32[16,16,384]{2,1,0:T(8,128)}, bf16[16,512,256]{2,1,0:T(8,128)(2,1)}) custom-call(f32[16,24,384]{2,1,0:T(8,128)} %pad_maximum_fusion.7.msg, bf16[512,256]{1,0:T(8,128)(2,1)} %pad_maximum_fusion.11.kv), custom_call_target="tpu_custom_call" | custom-call | tf_op jit(solution)/shard_map/front_exchange/pallas_call | solution.py:28
  99.1 4.1 flash_forward.1
  111.9 4.0 fusion.13
  130.9 40.5 %mixer_exchange.1 = (bf16[8,64,2176]{2,1,0:T(8,128)(2,1)}, f32[64,2048]{1,0:T(8,128)}) custom-call(bf16[8,64,2176]{2,1,0:T(8,128)(2,1)} %bitcast.247, bf16[64,2048]{1,0:T(8,128)(2,1)} %get-tuple-element.215.source, f32[1,2048]{1,0:T(1,128)} %get-tuple-element.199.gain, bf16[128,2048]{1,0:T(8,128)(2,1)} %b_out.1), custom_call_target="tpu_custom_call" | custom-call | tf_op jit(solution)/shard_map/mixer_exchange/pallas_call | solution.py:28
  171.4 5.3 fusion.27
  185.0 12.9 %convolution_convert_fusion.2 = bf16[512,2048]{1,0:T(8,128)(2,1)S(1)} fusion(bf16[2048,1024]{1,0:T(8,128)(2,1)S(1)} %bitcast.253, bf16[512,512]{0,1:T(8,128)(2,1)S(1)} %get-tuple-element.170, bf16[512,512]{0,1:T(8,128)(2,1)S(1)} %get-tuple-element.169), kind=kOutput, calls=%fused_computation.22 | convolution fusion | flops 2150629376 | bytes 7340032 | tf_op jit(solution)/shard_map/dot_general | solution.py:163
  200.9 65.5 %mlp_exchange.1 = (bf16[8,64,4352]{2,1,0:T(8,128)(2,1)}, f32[64,2048]{1,0:T(8,128)}, f32[1,2048]{1,0:T(1,128)}) custom-call(bf16[8,64,4352]{2,1,0:T(8,128)(2,1)} %bitcast.245, f32[64,2048]{1,0:T(8,128)} %get-tuple-element.44.resid, f32[1,2048]{1,0:T(1,128)} %get-tuple-element.199.gain, bf16[64,2048]{1,0:T(8,128)(2,1)} %get-tuple-element.214.out_grad, ...), custom_call_target="tpu_custom_call" | custom-call | tf_op jit(solution)/shard_map/mlp_exchange/pallas_call | solution.py:28
  266.4 4.4 convolution_convert_fusion.4
  271.0 3.6 fusion.10
  280.7 3.6 convolution_convert_fusion
  284.3 5.8 maximum_maximum_fusion
  290.2 3.6 fusion.14
  301.6 6.1 %flash_backward.1 = (f32[128,512]{1,0:T(8,128)}, bf16[16,512,256]{2,1,0:T(8,128)(2,1)}) custom-call(s32[2]{0:T(128)} %pad_add_fusion.at, bf16[128,512]{1,0:T(8,128)(2,1)} %copy.260.q_t, bf16[512,128]{1,0:T(8,128)(2,1)} %get-tuple-element.183.q, bf16[16,512,256]{2,1,0:T(8,128)(2,1)} %get-tuple-element.41.kv, s32[1,512]{1,0:T(1,128)} %bitcast.303, ...), custom_call_target="tpu_custom_call" | custom-call | tf_op jit(solution)/shard_map/flash_backward/pallas_call | solution.py:619
  307.8 60.9 %back_exchange.1 = (f32[16,16,384]{2,1,0:T(8,128)}, f32[256,256]{1,0:T(8,128)}) custom-call(f32[16,24,384]{2,1,0:T(8,128)} %pad_maximum_fusion.6.msg, bf16[16,512,256]{2,1,0:T(8,128)(2,1)} %get-tuple-element.47.dkv), custom_call_target="tpu_custom_call" | custom-call | tf_op jit(solution)/shard_map/back_exchange/pallas_call | solution.py:28
  376.4 4.3 fusion.12
  383.0 4.6 convert_multiply_fusion.3
  392.1 5.9 multiply_reduce_fusion
  436.2 45.3 %input_exchange.1 = (bf16[8,64,2304]{2,1,0:T(8,128)(2,1)}, f32[8,8,2048]{2,1,0:T(8,128)}, bf16[512,128]{1,0:T(8,128)(2,1)}) custom-call(bf16[8,64,2304]{2,1,0:T(8,128)(2,1)} %bitcast.246, bf16[8,512,128]{2,1,0:T(8,128)(2,1)} %maximum_bitcast_fusion.part_two, bf16[64,2048]{1,0:T(8,128)(2,1)} %get-tuple-element.215.source, f32[1,2048]{1,0:T(1,128)} %copy-done.70, ...), custom_call_target="tpu_custom_call" | custom-call | tf_op jit(solution)/shard_map/input_exchange/pallas_call | solution.py:28
  499.9 3.8 maximum_maximum_fusion.1.big
  503.8 55.1 %tail_exchange.1 = (f32[144,1024]{1,0:T(8,128)}, f32[256,128]{1,0:T(8,128)}, f32[8,152,128]{2,1,0:T(8,128)}, f32[8,128]{1,0:T(8,128)}) custom-call(bf16[16,144,1024]{2,1,0:T(8,128)(2,1)} %maximum_maximum_fusion.1.big, bf16[16,256,128]{2,1,0:T(8,128)(2,1)} %copy-done.18, f32[8,128]{1,0:T(8,128)} %select_maximum_fusion.head), custom_call_target="tpu_custom_call" | custom-call | tf_op jit(solution)/shard_map/tail_exchange/pallas_call | solution.py:28
  572.0 4.3 slice_convert_fusion.1
  (393 shorter events, 172.7 us)
Async XLA Ops:
  7.2 170.6 %copy-start = (bf16[512,2048]{1,0:T(8,128)(2,1)S(1)}, bf16[512,2048]{1,0:T(8,128)(2,1)}, u32[]{:S(2)}) copy-start(bf16[512,2048]{1,0:T(8,128)(2,1)} %param.30) | copy-start | bytes 6291460
  7.2 571.6 %reduce-scatter.5.cloned.1.call-start = ((), (), s32[]{:S(2)}) async-start(), calls=%async_computation.2 | async-start | bytes 2228224 | tf_op jit(solution)/shard_map/reduce_scatter | solution.py:877
  7.3 41.7 %copy-start.85 = (s32[128]{0:T(128)}, s32[128]{0:T(128)S(1)}, u32[]{:S(2)}) copy-start(s32[128]{0:T(128)S(1)} %and_select_fusion) | copy-start | bytes 1540
  9.1 13.1 %copy-start.73 = (s32[512]{0:T(512)}, s32[512]{0:T(512)S(1)}, u32[]{:S(2)}) copy-start(s32[512]{0:T(512)S(1)} %get-tuple-element.163) | copy-start | bytes 6148
  9.1 39.9 %copy-start.76 = (s32[512]{0:T(512)}, s32[512]{0:T(512)S(1)}, u32[]{:S(2)}) copy-start(s32[512]{0:T(512)S(1)} %get-tuple-element.164) | copy-start | bytes 6148
  15.4 34.3 %copy-start.81 = (pred[512]{0:T(512)(128)(4,1)}, pred[512]{0:T(512)(128)(4,1)S(1)}, u32[]{:S(2)}) copy-start(pred[512]{0:T(512)(128)(4,1)S(1)} %get-tuple-element.202) | copy-start | bytes 1540
  24.2 25.5 %copy-start.31 = (f32[512,6]{1,0:T(8,128)}, f32[512,6]{1,0:T(8,128)S(1)}, u32[]{:S(2)}) copy-start(f32[512,6]{1,0:T(8,128)S(1)} %convolution_add_fusion.5) | copy-start | bytes 36868
  25.7 24.1 %copy-start.80 = (f32[6]{0:T(128)}, f32[6]{0:T(128)S(1)}, u32[]{:S(2)}) copy-start(f32[6]{0:T(128)S(1)} %slice_reduce_fusion) | copy-start | bytes 76
  25.8 23.9 %copy-start.20 = (f32[512,6]{1,0:T(8,128)}, f32[512,6]{1,0:T(8,128)S(1)}, u32[]{:S(2)}) copy-start(f32[512,6]{1,0:T(8,128)S(1)} %copy.254) | copy-start | bytes 36868
  42.3 6.6 %copy-start.4 = (bf16[512,2048]{1,0:T(8,128)(2,1)S(1)}, bf16[512,2048]{1,0:T(8,128)(2,1)}, u32[]{:S(2)}) copy-start(bf16[512,2048]{1,0:T(8,128)(2,1)} %copy-done.2) | copy-start | bytes 6291460
  42.3 6.6 %copy-start.42 = (bf16[2048,128]{1,0:T(8,128)(2,1)S(1)}, bf16[2048,128]{1,0:T(8,128)(2,1)}, u32[]{:S(2)}) copy-start(bf16[2048,128]{1,0:T(8,128)(2,1)} %a_sh.1) | copy-start | bytes 1572868
  99.1 10.2 %slice-start = ((bf16[512,896]{1,0:T(8,128)(2,1)}), bf16[512,384]{1,0:T(8,128)(2,1)S(1)}, s32[]{:S(2)}) async-start(bf16[512,896]{1,0:T(8,128)(2,1)} %copy-done.7), calls=%async_computation.4 | async-start | bytes 786432 | tf_op jit(solution)/shard_map/slice | solution.py:777
  115.9 6.3 %copy-start.25 = (f32[16,16,384]{2,1,0:T(8,128)S(1)}, f32[16,16,384]{2,1,0:T(8,128)}, u32[]{:S(2)}) copy-start(f32[16,16,384]{2,1,0:T(8,128)} %get-tuple-element.40) | copy-start | bytes 1179652
  200.9 65.5 %copy-start.98 = (bf16[512,384]{1,0:T(8,128)(2,1)S(1)}, bf16[512,384]{1,0:T(8,128)(2,1)}, u32[]{:S(2)}) copy-start(bf16[512,384]{1,0:T(8,128)(2,1)} %copy-done.97) | copy-start | bytes 1179652
  270.9 309.7 %reduce-scatter.7.cloned.1.call-start = ((), (), s32[]{:S(2)}) async-start(), calls=%async_computation.3 | async-start | bytes 7102464
  307.8 63.6 %copy-start.24 = (bf16[512,384]{1,0:T(8,128)(2,1)S(1)}, bf16[512,384]{1,0:T(8,128)(2,1)}, u32[]{:S(2)}) copy-start(bf16[512,384]{1,0:T(8,128)(2,1)} %get-tuple-element.179) | copy-start | bytes 1179652
  368.7 7.7 %copy-start.75 = (f32[6,512]{1,0:T(8,128)S(1)}, f32[6,512]{1,0:T(8,128)}, u32[]{:S(2)}) copy-start(f32[6,512]{1,0:T(8,128)} %copy-done.74) | copy-start | bytes 36868
  369.8 10.9 %copy-start.27 = (bf16[512,128]{1,0:T(8,128)(2,1)}, bf16[512,128]{1,0:T(8,128)(2,1)S(1)}, u32[]{:S(2)}) copy-start(bf16[512,128]{1,0:T(8,128)(2,1)S(1)} %get-tuple-element.192) | copy-start | bytes 393220
  376.4 6.6 %copy-start.11 = (f32[512,384]{1,0:T(8,128)S(1)}, f32[512,384]{1,0:T(8,128)}, u32[]{:S(2)}) copy-start(f32[512,384]{1,0:T(8,128)} %copy.256) | copy-start | bytes 2359300
  376.4 6.6 %copy-start.82 = (f32[384]{0:T(512)S(1)}, f32[384]{0:T(512)}, u32[]{:S(2)}) copy-start(f32[384]{0:T(512)} %mul.311) | copy-start | bytes 4612
  392.1 9.0 %copy-start.21 = (f32[512,6]{1,0:T(8,128)S(1)}, f32[512,6]{1,0:T(8,128)}, u32[]{:S(2)}) copy-start(f32[512,6]{1,0:T(8,128)} %copy-done.20) | copy-start | bytes 36868
  481.6 7.1 %copy-start.5 = (bf16[512,2048]{1,0:T(8,128)(2,1)S(1)}, bf16[512,2048]{1,0:T(8,128)(2,1)}, u32[]{:S(2)}) copy-start(bf16[512,2048]{1,0:T(8,128)(2,1)} %copy-done.2) | copy-start | bytes 6291460
  481.6 7.1 %copy-start.44 = (bf16[512,128]{1,0:T(8,128)(2,1)S(1)}, bf16[512,128]{1,0:T(8,128)(2,1)}, u32[]{:S(2)}) copy-start(bf16[512,128]{1,0:T(8,128)(2,1)} %get-tuple-element.54) | copy-start | bytes 393220
  579.7 7.0 %copy-start.1 = (bf16[512,2048]{1,0:T(8,128)(2,1)S(1)}, bf16[512,2048]{1,0:T(8,128)(2,1)}, u32[]{:S(2)}) copy-start(bf16[512,2048]{1,0:T(8,128)(2,1)} %param.30) | copy-start | bytes 6291460
  (83 other events, 251.2 us)
Sparse Core Ops, SparseCore 0:
  271.0 91.6 reduce-scatter.4
  366.6 78.4 reduce-scatter.6
